TPU v7x, 32 devices: a whole 2x2x4 slice. The times are simulated.
32 devices in a mesh: shard: 4 (over y, x), rep: 8 (over z, core).
Axes of the slice: x: 2, y: 2, z: 4, core: 2. Of those that a mesh axis runs over, the one named last changes fastest.
Arguments:
- tokens: bfloat16 [8, 1024, 1600], P('rep', 'shard'), may hold values from -6 to 6
- cotangent: bfloat16 [8, 1024, 1600], P('rep', 'shard'), may hold values from -6 to 6
- lengths: int32 [8, 3], P('rep'), may hold values from 1 to 4, 8 in all within a row
- attn_weight: bfloat16 [1600, 4800], P('shard'), may hold values from -0.15625 to 0.15625
- query_bias: bfloat16 [1600], P('shard'), may hold values from -1.75 to 1.75
- value_bias: bfloat16 [1600], P('shard'), may hold values from -0.125 to 0.125
- proj_weight: bfloat16 [1600, 1600], P('shard'), may hold values from -2.5 to 2.5
- proj_bias: bfloat16 [1600], P('shard'), may hold values from -1.75 to 1.75
- ln1_gain: bfloat16 [1600], P('shard'), may hold values from 0.25 to 1.75
- ln1_bias: bfloat16 [1600], P('shard'), may hold values from -1.75 to 1.75
- ln2_gain: bfloat16 [1600], P('shard'), may hold values from 0.25 to 1.75
- ln2_bias: bfloat16 [1600], P('shard'), may hold values from -1.75 to 1.75
- fc_weight: bfloat16 [1600, 6400], P('shard'), may hold values from -0.15625 to 0.15625
- fc_bias: bfloat16 [6400], P('shard'), may hold values from -3 to 3
- out_weight: bfloat16 [6400, 1600], P('shard'), may hold values from -0.109375 to 0.109375
- out_bias: bfloat16 [1600], P('shard'), may hold values from -1.75 to 1.75
Outputs:
- output: bfloat16 [8, 1024, 1600], P('rep', 'shard')
- input_grad: bfloat16 [8, 1024, 1600], P('rep', 'shard')
- grad_attn_weight: float32 [1600, 4800], P('shard')
- grad_query_bias: float32 [1600], P('shard')
- grad_value_bias: float32 [1600], P('shard')
- grad_proj_weight: float32 [1600, 1600], P('shard')
- grad_proj_bias: float32 [1600], P('shard')
- grad_ln1_gain: float32 [1600], P('shard')
- grad_ln1_bias: float32 [1600], P('shard')
- grad_ln2_gain: float32 [1600], P('shard')
- grad_ln2_bias: float32 [1600], P('shard')
- grad_fc_weight: float32 [1600, 6400], P('shard')
- grad_fc_bias: float32 [6400], P('shard')
- grad_out_weight: float32 [6400, 1600], P('shard')
- grad_out_bias: float32 [1600], P('shard')
Inputs may be any that keep to these rules, and one draw needn't show every extreme that they name: Each row of lengths sums to 8; a sequence holds 4 * 32 times its entry in tokens, an equal share on each device of its group; the largest entry of every row is reached.
All inputs are finite; a program needn't handle non-finite values.
Results may differ from a plain program's by a relative error of at most 0.02.
Values may be sent and summed in bfloat16 or wider, within the bound.
No kernel may reach another device: no remote copies, remote signals or barrier semaphores. Data moves between devices by JAX's collectives and lax.ppermute only.
A program may use at most 384 MiB of HBM per device.

v0:
```python
import functools
import math

import jax
import jax.numpy as jnp
from jax import lax
from jax.experimental import pallas as pl
from jax.experimental.pallas import tpu as pltpu
from jax.sharding import PartitionSpec as P

D = 1600
HEADS = 25
HD = 64
UNIT = 32
LANES = 128
NEG = -1e30
VEC_ROWS = 16
BF = jnp.bfloat16
F32 = jnp.float32


def dot(left, right, dims):
    return lax.dot_general(left, right, (dims, ((), ())), preferred_element_type=F32)


def rows_dot(left, right):
    return dot(left, right, ((0,), (0,)))


def cols_dot(left, right):
    return dot(left, right, ((1,), (1,)))


def normalize(values):
    center = values - jnp.mean(values, axis=-1, keepdims=True)
    spread = jnp.mean(center * center, axis=-1, keepdims=True)
    inv = lax.rsqrt(spread + 1e-05)
    return center * inv, inv


def place_blocks(info_ref, shards, units):
    b0, b1, b2, me = info_ref[0], info_ref[1], info_ref[2], info_ref[3]
    e0, e1 = b0, b0 + b1
    places = []
    for d in range(shards):
        s = jnp.bitwise_xor(me, d)
        for u in range(units):
            first = jnp.where(u < e0, 0, jnp.where(u < e1, e0, e1))
            span = jnp.where(u < e0, b0, jnp.where(u < e1, b1, b2))
            places.append((d * units + u, first * shards + s * span + (u - first)))
    return places, e0, e1


def head_lanes(tile_rows, half):
    lane = lax.broadcasted_iota(jnp.int32, (tile_rows, LANES), 1)
    return (lane < HD) if half == 0 else (lane >= HD)


def window_scores(q, k, rows, width):
    scores = cols_dot(q, k)
    row = lax.broadcasted_iota(jnp.int32, (rows, width * rows), 0)
    col = lax.broadcasted_iota(jnp.int32, (rows, width * rows), 1)
    return jnp.where(col <= row + (width - 1) * rows, scores, NEG)


def fwd_kernel(shards, units, heads, info_ref, qkv_ref, out_ref, perm, mixed):
    block = UNIT
    rows = shards * block
    main = heads * HD
    places, e0, e1 = place_blocks(info_ref, shards, units)
    for src, dst in places:
        at = pl.ds(pl.multiple_of(dst * block, block), block)
        perm[at, :] = qkv_ref[src * block : (src + 1) * block, :]

    def unit(i, carry):
        first = jnp.where(i < e0, 0, jnp.where(i < e1, e0, e1))
        q_at = pl.ds(pl.multiple_of(i * rows, rows), rows)
        for width in range(1, 5):

            @pl.when(i - first + 1 == width)
            def _():
                k_at = pl.ds(pl.multiple_of(first * rows, rows), width * rows)

                def attend(q, k, v):
                    scores = window_scores(q * BF(0.125), k, rows, width)
                    top = jnp.max(scores, axis=1, keepdims=True)
                    probs = jnp.exp(scores - top)
                    total = jnp.sum(probs, axis=1, keepdims=True)
                    return dot(probs.astype(BF), v, ((1,), (0,))) / total

                for tile in range(main // LANES):
                    lanes = slice(tile * LANES, (tile + 1) * LANES)
                    k_lanes = slice(main + lanes.start, main + lanes.stop)
                    v_lanes = slice(2 * main + lanes.start, 2 * main + lanes.stop)
                    q, k, v = perm[q_at, lanes], perm[k_at, k_lanes], perm[k_at, v_lanes]
                    low = head_lanes(rows, 0)
                    zero = jnp.zeros_like(q)
                    left = attend(jnp.where(low, q, zero), k, v)
                    right = attend(jnp.where(low, zero, q), k, v)
                    mixed[q_at, lanes] = jnp.where(low, left, right).astype(BF)
                if main % LANES:
                    lanes = main - HD
                    mixed[q_at, lanes:main] = attend(
                        perm[q_at, lanes:main],
                        perm[k_at, main + lanes : 2 * main],
                        perm[k_at, 2 * main + lanes : 3 * main],
                    ).astype(BF)
                base = 3 * main
                mixed[q_at, main : main + HD] = attend(
                    perm[q_at, base : base + HD],
                    perm[k_at, base + HD : base + 2 * HD],
                    perm[k_at, base + 2 * HD : base + 3 * HD],
                ).astype(BF)

        return carry

    lax.fori_loop(0, units, unit, 0)
    for src, dst in places:
        at = pl.ds(pl.multiple_of(dst * block, block), block)
        out_ref[src * block : (src + 1) * block, :] = mixed[at, :]


def bwd_kernel(
    shards, units, heads, info_ref, qkv_ref, dmix_ref, out_ref, perm, dperm, dq_acc, dk_acc, dv_acc
):
    block = UNIT
    rows = shards * block
    main = heads * HD
    places, e0, e1 = place_blocks(info_ref, shards, units)
    for src, dst in places:
        at = pl.ds(pl.multiple_of(dst * block, block), block)
        perm[at, :] = qkv_ref[src * block : (src + 1) * block, :]
        dperm[at, :] = dmix_ref[src * block : (src + 1) * block, :]
    dk_acc[...] = jnp.zeros_like(dk_acc)
    dv_acc[...] = jnp.zeros_like(dv_acc)

    def unit(i, carry):
        first = jnp.where(i < e0, 0, jnp.where(i < e1, e0, e1))
        q_at = pl.ds(pl.multiple_of(i * rows, rows), rows)
        for width in range(1, 5):

            @pl.when(i - first + 1 == width)
            def _():
                k_at = pl.ds(pl.multiple_of(first * rows, rows), width * rows)

                def pull(q, k, v, g):
                    q = q * BF(0.125)
                    scores = window_scores(q, k, rows, width)
                    top = jnp.max(scores, axis=1, keepdims=True)
                    probs = jnp.exp(scores - top)
                    total = jnp.sum(probs, axis=1, keepdims=True)
                    probs = probs * (1.0 / total)
                    d_probs = cols_dot(g, v)
                    delta = jnp.sum(probs * d_probs, axis=1, keepdims=True)
                    d_scores = (probs * (d_probs - delta)).astype(BF)
                    d_q = dot(d_scores, k, ((1,), (0,))) * 0.125
                    return d_q, rows_dot(d_scores, q), rows_dot(probs.astype(BF), g)

                for tile in range(main // LANES):
                    lanes = slice(tile * LANES, (tile + 1) * LANES)
                    k_lanes = slice(main + lanes.start, main + lanes.stop)
                    v_lanes = slice(2 * main + lanes.start, 2 * main + lanes.stop)
                    q, k, v = perm[q_at, lanes], perm[k_at, k_lanes], perm[k_at, v_lanes]
                    g = dperm[q_at, lanes]
                    low = head_lanes(rows, 0)
                    zero = jnp.zeros_like(q)
                    dq0, dk0, dv0 = pull(jnp.where(low, q, zero), k, v, jnp.where(low, g, zero))
                    dq1, dk1, dv1 = pull(jnp.where(low, zero, q), k, v, jnp.where(low, zero, g))
                    dq_acc[q_at, lanes] = jnp.where(low, dq0, dq1).astype(BF)
                    dk_acc[k_at, lanes] += dk0 + dk1
                    dv_acc[k_at, lanes] += dv0 + dv1
                extra = [(main, 3 * main, 3 * main + HD, 3 * main + 2 * HD)]
                if main % LANES:
                    extra.append((main - HD, main - HD, 2 * main - HD, 3 * main - HD))
                for own, q_lane, k_lane, v_lane in extra:
                    dq0, dk0, dv0 = pull(
                        perm[q_at, q_lane : q_lane + HD],
                        perm[k_at, k_lane : k_lane + HD],
                        perm[k_at, v_lane : v_lane + HD],
                        dperm[q_at, own : own + HD],
                    )
                    dq_acc[q_at, own : own + HD] = dq0.astype(BF)
                    dk_acc[k_at, own : own + HD] += dk0
                    dv_acc[k_at, own : own + HD] += dv0

        return carry

    lax.fori_loop(0, units, unit, 0)
    for src, dst in places:
        at = pl.ds(pl.multiple_of(dst * block, block), block)
        to = slice(src * block, (src + 1) * block)
        for part, acc in enumerate((dq_acc, dk_acc, dv_acc)):
            got = acc[at, :].astype(BF)
            out_ref[to, part * main : (part + 1) * main] = got[:, :main]
            lane = 3 * main + part * HD
            out_ref[to, lane : lane + HD] = got[:, main:]


def vmem_call(kernel, out_shape, scratch, cost, inputs):
    return pl.pallas_call(
        kernel,
        out_shape=out_shape,
        in_specs=[pl.BlockSpec(memory_space=pltpu.SMEM)]
        + [pl.BlockSpec(memory_space=pltpu.VMEM)] * (len(inputs) - 1),
        out_specs=pl.BlockSpec(memory_space=pltpu.VMEM),
        scratch_shapes=scratch,
        compiler_params=pltpu.CompilerParams(vmem_limit_bytes=48 << 20),
        cost_estimate=cost,
    )(*inputs)


def attention_fwd(info, qkv, shards, heads):
    total, width = qkv.shape
    units = total // (shards * UNIT)
    own = (heads + 1) * HD
    return vmem_call(
        functools.partial(fwd_kernel, shards, units, heads),
        jax.ShapeDtypeStruct((total, own), BF),
        [pltpu.VMEM((total, width), BF), pltpu.VMEM((total, own), BF)],
        pl.CostEstimate(flops=1, bytes_accessed=1, transcendentals=0),
        (info, qkv),
    )


def attention_bwd(info, qkv, d_mixed, shards, heads):
    total, width = qkv.shape
    units = total // (shards * UNIT)
    own = (heads + 1) * HD
    return vmem_call(
        functools.partial(bwd_kernel, shards, units, heads),
        jax.ShapeDtypeStruct((total, width), BF),
        [
            pltpu.VMEM((total, width), BF),
            pltpu.VMEM((total, own), BF),
            pltpu.VMEM((total, own), BF),
            pltpu.VMEM((total, own), F32),
            pltpu.VMEM((total, own), F32),
        ],
        pl.CostEstimate(flops=1, bytes_accessed=1, transcendentals=0),
        (info, qkv, d_mixed),
    )


def on_place(me, core, shards, run):
    for m in range(shards):
        for c in range(2):

            @pl.when((me == m) & (core == c))
            def _():
                run(m, c)


def attn_columns(value, j, heads):
    main = heads * HD
    first = D // main * main
    parts = [value[:, p * D + j * main : p * D + (j + 1) * main] for p in range(3)]
    parts += [value[:, p * D + first : (p + 1) * D] for p in range(3)]
    return jnp.concatenate(parts, axis=1)


def fc_columns(value, j, width):
    return value[:, j * width : (j + 1) * width]


def pack_kernel(shards, half, step, columns, at_ref, dep_ref, weight_ref, *outs):
    del dep_ref

    def run(m, c):
        outs[0][...] = columns(weight_ref, m)
        for d in range(1, shards):
            piece = columns(weight_ref.at[c * step : c * step + half], m ^ d)
            outs[d][...] = piece

    on_place(at_ref[0], at_ref[1], shards, run)


def pack_attn_kernel(shards, half, step, heads, count, at_ref, weight_ref, *refs):
    sources, outs = refs[:count], refs[count : count + shards]
    vectors, sems = refs[count + shards : 2 * count + shards], refs[2 * count + shards]
    length = vectors[0].shape[0]
    copies = [
        pltpu.make_async_copy(source, vector, sems.at[i])
        for i, (source, vector) in enumerate(zip(sources, vectors))
    ]
    for copy in copies:
        copy.start()

    def run(m, c):
        outs[0][: shards_rows(outs[0]), :] = attn_columns(weight_ref, m, heads)
        for d in range(1, shards):
            outs[d][:half, :] = attn_columns(weight_ref.at[c * step : c * step + half], m ^ d, heads)

    def shards_rows(ref):
        return ref.shape[0] - VEC_ROWS

    on_place(at_ref[0], at_ref[1], shards, run)
    for copy in copies:
        copy.wait()
    width = outs[0].shape[1]
    block = jnp.concatenate(
        [v[...].astype(F32).reshape(1, length) for v in vectors]
        + [jnp.zeros((VEC_ROWS - count, length), F32)],
        axis=0,
    )
    block = jnp.concatenate(
        [block, jnp.zeros((VEC_ROWS, width - length), F32)], axis=1
    ).astype(BF)
    for out in outs:
        out[out.shape[0] - VEC_ROWS :, :] = block


def place_attn_kernel(shards, half, step, rows, count, at_ref, *refs):
    own, mine, other = refs[0], refs[1:shards], refs[shards]
    out, vec = refs[shards + 1 :]

    def run(m, c):
        out[m * rows : (m + 1) * rows, :] = own[:rows]
        for d in range(1, shards):
            base = (m ^ d) * rows
            a, b = mine[d - 1][:half], other[d - 1]
            low, high = (a, b) if c == 0 else (b, a)
            out[base : base + step, :] = low[:step]
            out[base + step : base + rows, :] = high
        for j in range(shards):
            ref, at = (own, rows) if j == m else (mine[(j ^ m) - 1], half)
            vec[:, j * rows : (j + 1) * rows] = ref[at : at + VEC_ROWS, :rows].astype(F32)[:count]

    on_place(at_ref[0], at_ref[1], shards, run)


def place_kernel(shards, half, step, rows, at_ref, *refs):
    own, mine, other, out = refs[0], refs[1:shards], refs[shards], refs[shards + 1]

    def run(m, c):
        out[m * rows : (m + 1) * rows, :] = own[...]
        for d in range(1, shards):
            base = (m ^ d) * rows
            low, high = (mine[d - 1][...], other[d - 1]) if c == 0 else (other[d - 1], mine[d - 1][...])
            out[base : base + step, :] = low[:step]
            out[base + step : base + rows, :] = high

    on_place(at_ref[0], at_ref[1], shards, run)


def pack_part_kernel(shards, length, stride, columns, at_ref, weight_ref, *outs):
    part = pl.ds(pl.multiple_of(at_ref[2] * stride, 16), length)
    for m in range(shards):

        @pl.when(at_ref[0] == m)
        def _():
            outs[0][...] = columns(weight_ref, m)
            for d in range(1, shards):
                outs[d][...] = columns(weight_ref.at[part], m ^ d)


def place_part_kernel(shards, length, stride, rows, at_ref, own, mine, near, across, out):
    me, q = at_ref[0], at_ref[2]
    out[pl.ds(pl.multiple_of(me * rows, 16), rows), :] = own[...]
    size = (shards - 1) * length
    for d in range(1, shards):
        base = jnp.bitwise_xor(me, d) * rows
        for flip, ref, first in ((0, mine, 0), (2, near, 0), (1, across, 0), (3, across, size)):
            to = base + jnp.bitwise_xor(q, flip) * stride
            row = first + (d - 1) * length
            out[pl.ds(pl.multiple_of(to, 16), length), :] = ref[row : row + length, :]


def unpack_kernel(shards, half, step, places, count, at_ref, *refs):
    mine, other, outs = refs[:count], refs[count : 2 * count], refs[2 * count :]

    def run(m, c):
        for d in range(shards):
            for index, where, part, row, low, high in places(m, d):
                out, width = outs[index], high - low
                a = mine[part][row : row + half, low:high]
                b = other[part][row : row + half, low:high]
                first, second = (a, b) if c == 0 else (b, a)
                out[:step, where : where + width] = first[:step].astype(F32)
                out[step:, where : where + width] = second.astype(F32)

    on_place(at_ref[0], at_ref[1], shards, run)


def local_call(kernel, out_shape, cost_bytes, at, *inputs, anywhere=(), scratch=()):
    vmem = pl.BlockSpec(memory_space=pltpu.VMEM)
    hbm = pl.BlockSpec(memory_space=pltpu.HBM)
    specs = [hbm if i in anywhere else vmem for i in range(len(inputs))]
    return pl.pallas_call(
        kernel,
        out_shape=out_shape,
        in_specs=[pl.BlockSpec(memory_space=pltpu.SMEM)] + specs,
        out_specs=jax.tree.map(lambda _: vmem, out_shape),
        scratch_shapes=list(scratch),
        compiler_params=pltpu.CompilerParams(vmem_limit_bytes=48 << 20),
        cost_estimate=pl.CostEstimate(flops=1, bytes_accessed=1, transcendentals=0),
    )(at, *inputs)


def body(
    tokens,
    cotangent,
    lengths,
    attn_weight,
    query_bias,
    value_bias,
    proj_weight,
    proj_bias,
    ln1_gain,
    ln1_bias,
    ln2_gain,
    ln2_bias,
    fc_weight,
    fc_bias,
    out_weight,
    out_bias,
):
    n = lax.axis_size("shard")
    planes = lax.axis_size("plane")
    me = lax.axis_index("shard")
    core = lax.axis_index("core")
    heads = (HEADS - 1) // n
    main = heads * HD
    spare = D - n * main
    own_rows = attn_weight.shape[0]
    own_ff = fc_bias.shape[0]
    rows = tokens.shape[1]
    half = -(-own_rows // 32) * 16
    step = own_rows - half
    quarter = lax.axis_index("plane") % 2 * 2 + core
    at = jnp.stack([me, core, quarter]).astype(jnp.int32)

    def swap(value, d):
        return lax.ppermute(value, "shard", [(i, i ^ d) for i in range(n)])

    def swap_plane(value):
        return lax.ppermute(value, "plane", [(i, i ^ 1) for i in range(planes)])

    def swap_core(value):
        return lax.ppermute(value, "core", [(0, 1), (1, 0)])

    def gather_near(value):
        if n != 4:
            return [swap(value, d) for d in range(1, n)]
        return [swap(value, 1), swap(value, 2)]

    def gather_far(value, near):
        if n != 4:
            return [value] + near
        one, two = near
        cut = value.shape[0] // 32 * 16
        three = jnp.concatenate([swap(one[:cut], 2), swap(two[cut:], 1)], axis=0)
        return [value, one, two, three]

    def gather(value):
        return gather_far(value, gather_near(value))

    def pick(stacked, index):
        return lax.dynamic_index_in_dim(stacked, index, 0, keepdims=False)

    def natural(pieces):
        stacked = jnp.stack(pieces)
        return [pick(stacked, me ^ j) for j in range(n)]

    def after(value, *deps):
        return lax.optimization_barrier((value, deps))[0]

    def block(value, d):
        return value[d * rows : (d + 1) * rows]

    def place(own, mine):
        other = swap_core(jnp.stack(mine))
        return local_call(
            functools.partial(place_kernel, n, half, step, own_rows),
            jax.ShapeDtypeStruct((n * own_rows, own.shape[1]), BF),
            n * own.size * 4,
            at,
            own,
            *mine,
            other,
        )

    def pack(weight, columns, width, dep):
        shapes = [jax.ShapeDtypeStruct((own_rows, width), BF)]
        shapes += [jax.ShapeDtypeStruct((half, width), BF)] * (n - 1)
        return local_call(
            functools.partial(pack_kernel, n, half, step, columns),
            shapes,
            weight.size * 2,
            at,
            dep,
            weight,
            anywhere=(0,),
        )

    def reduce_rows(parts, *deps):
        got = after([swap(parts[d].astype(BF), d) for d in range(1, n)], *deps)
        total = parts[0].astype(F32)
        for part in got:
            total = total + part.astype(F32)
        return total

    def core_halves(parts):
        keep = lax.dynamic_slice_in_dim(parts, core * step, half, 1)
        give = lax.dynamic_slice_in_dim(parts, (1 - core) * step, half, 1)
        return (keep.astype(F32) + swap_core(give).astype(F32)).astype(BF)

    vectors = (
        query_bias, value_bias, proj_bias, ln1_gain, ln1_bias, ln2_gain, ln2_bias, out_bias
    )
    tokens_near = gather_near(tokens[0])
    attn_width = 3 * (main + spare)
    attn_sent = local_call(
        functools.partial(pack_attn_kernel, n, half, step, heads, len(vectors)),
        [jax.ShapeDtypeStruct((own_rows + VEC_ROWS, attn_width), BF)]
        + [jax.ShapeDtypeStruct((half + VEC_ROWS, attn_width), BF)] * (n - 1),
        attn_weight.size * 2,
        at,
        attn_weight,
        *vectors,
        anywhere=range(1, len(vectors) + 1),
        scratch=[pltpu.VMEM((own_rows,), BF)] * len(vectors)
        + [pltpu.SemaphoreType.DMA((len(vectors),))],
    )
    attn_got = [swap(attn_sent[d], d) for d in range(1, n)]
    attn_got, tokens_near = after((attn_got, tokens_near))
    attn_other = swap_core(jnp.stack([piece[:half] for piece in attn_got]))
    tokens_parts = gather_far(tokens[0], tokens_near)
    w_attn, small = local_call(
        functools.partial(place_attn_kernel, n, half, step, own_rows, len(vectors)),
        [
            jax.ShapeDtypeStruct((D, attn_width), BF),
            jax.ShapeDtypeStruct((len(vectors), D), F32),
        ],
        D * attn_width * 4,
        at,
        attn_sent[0],
        *attn_got,
        attn_other,
    )
    b_query, b_value, b_proj, gain_one, bias_one, gain_two, bias_two, b_out = [
        small[i] for i in range(8)
    ]

    def my_columns(vector):
        return lax.dynamic_slice_in_dim(vector, me * main, main, 0), vector[n * main :]

    q_main, q_spare = my_columns(b_query)
    v_main, v_spare = my_columns(b_value)
    qkv_bias = jnp.concatenate(
        [q_main, jnp.zeros_like(q_main), v_main, q_spare, jnp.zeros_like(q_spare), v_spare]
    )

    group_tokens = jnp.concatenate(tokens_parts, axis=0)
    proj_half = lax.dynamic_slice_in_dim(after(proj_weight, attn_got), core * step, half, 0)
    proj_near = gather_near(proj_half)
    own_cot = cotangent[0]
    cot_all = lax.all_gather(after(own_cot, attn_got, tokens_parts), "shard", axis=0, tiled=True)
    late_fc = after(fc_weight, attn_got)
    stride = own_rows // 64 * 16
    length = own_rows - 3 * stride
    by_parts = own_rows % 16 == 0 and stride > 0 and planes % 2 == 0
    if by_parts:
        fc_sent = local_call(
            functools.partial(
                pack_part_kernel, n, length, stride, lambda ref, j: fc_columns(ref, j, own_ff)
            ),
            [jax.ShapeDtypeStruct((own_rows, own_ff), BF)]
            + [jax.ShapeDtypeStruct((length, own_ff), BF)] * (n - 1),
            fc_weight.size * 2,
            at,
            late_fc,
        )
    else:
        fc_sent = pack(late_fc, lambda ref, j: fc_columns(ref, j, own_ff), own_ff, lengths)
    xhat_one, _ = normalize(group_tokens.astype(F32))
    normed = (xhat_one * gain_one + bias_one).astype(BF)
    qkv = (jnp.dot(normed, w_attn, preferred_element_type=F32) + qkv_bias).astype(BF)
    qkv, proj_near, fc_sent = after((qkv, proj_near, fc_sent))
    proj_parts = gather_far(proj_half, proj_near)
    fc_got = [swap(fc_sent[d], d) for d in range(1, n)]
    info = jnp.concatenate([lengths[0], me.astype(jnp.int32)[None]])
    mixed_heads = attention_fwd(info, qkv, n, heads)
    mixed_heads, proj_parts, fc_got = after((mixed_heads, proj_parts, fc_got))
    if by_parts:
        fc_mine = jnp.concatenate(fc_got)
        fc_near = swap_plane(fc_mine)
    got = [block(mixed_heads, 0)[:, :main]] + [
        swap(block(mixed_heads, d)[:, :main], d) for d in range(1, n)
    ]
    w_proj = place(proj_weight, proj_parts[1:])
    got, w_proj, cot_all = after((got, w_proj, cot_all))
    mixed_low = jnp.concatenate(natural(got) + [block(mixed_heads, 0)[:, main:]], axis=1)
    own_tokens = tokens[0].astype(F32)
    middle = own_tokens + jnp.dot(mixed_low, w_proj, preferred_element_type=F32) + b_proj
    xhat_two, inv_two = normalize(middle)
    own_normed_two = (xhat_two * gain_two + bias_two).astype(BF)
    normed_near = gather_near(own_normed_two)
    if by_parts:
        w_fc = local_call(
            functools.partial(place_part_kernel, n, length, stride, own_rows),
            jax.ShapeDtypeStruct((D, own_ff), BF),
            D * own_ff * 4,
            at,
            fc_sent[0],
            fc_mine,
            fc_near,
            swap_core(jnp.concatenate(after([fc_mine, fc_near], own_normed_two))),
        )
    else:
        w_fc = place(fc_sent[0], fc_got)
    cot_parts = [own_cot] + [
        lax.dynamic_slice_in_dim(cot_all, (me ^ d) * rows, rows, 0) for d in range(1, n)
    ]
    group_cot = jnp.concatenate(cot_parts, axis=0)
    d_active = cols_dot(group_cot, out_weight).astype(BF)
    normed_near, d_active = after((normed_near, d_active))
    normed_parts = gather_far(own_normed_two, normed_near)
    normed_two = jnp.concatenate(normed_parts, axis=0)

    def feed(part):
        hidden = jnp.dot(part, w_fc, preferred_element_type=F32) + fc_bias.astype(F32)
        inner = jnp.tanh(0.7978845608028654 * (hidden + 0.044715 * hidden * hidden * hidden))
        slope = 0.5 * (1.0 + inner) + 0.5 * hidden * (1.0 - inner * inner) * (
            0.7978845608028654 * (1.0 + 3 * 0.044715 * hidden * hidden)
        )
        return (0.5 * hidden * (1.0 + inner)).astype(BF), slope.astype(BF)

    fed = [feed(part) for part in normed_parts]
    active_parts = [a for a, _ in fed]
    active = jnp.concatenate(active_parts, axis=0)

    grad_out_weight = rows_dot(active, group_cot).astype(BF)
    sum_out_weight = lax.psum(grad_out_weight, ("plane", "core"))
    d_active = after(d_active, grad_out_weight)
    d_hidden_parts = [
        (block(d_active, d).astype(F32) * slope.astype(F32)).astype(BF)
        for d, (_, slope) in enumerate(fed)
    ]
    d_hidden = jnp.concatenate(d_hidden_parts, axis=0)
    e = reduce_rows([cols_dot(part, w_fc) for part in d_hidden_parts])
    e_gain = e * gain_two
    d_middle = own_cot.astype(F32) + inv_two * (
        e_gain
        - jnp.mean(e_gain, axis=-1, keepdims=True)
        - xhat_two * jnp.mean(e_gain * xhat_two, axis=-1, keepdims=True)
    )
    d_branch = d_middle.astype(BF)
    d_mixed = cols_dot(d_branch, w_proj).astype(BF)
    for_heads = jnp.stack([d_mixed[:, j * main : (j + 1) * main] for j in range(n)])
    last = d_mixed[:, n * main :]
    dmix_parts = [jnp.concatenate([pick(for_heads, me), last], axis=1)] + [
        swap(jnp.concatenate([pick(for_heads, me ^ d), last], axis=1), d) for d in range(1, n)
    ]

    grad_fc = rows_dot(normed_two, d_hidden).astype(BF).reshape(n, own_rows, own_ff)
    fc_halves = after(core_halves(grad_fc), dmix_parts)
    fc_parts = jnp.concatenate(
        [pick(fc_halves, me)] + [swap(pick(fc_halves, me ^ d), d) for d in range(1, n)]
    )
    fc_sum = lax.psum(fc_parts, "plane")
    grad_fc_bias = jnp.sum(d_hidden.astype(F32), axis=0)

    d_qkv = attention_bwd(info, qkv, jnp.concatenate(dmix_parts, axis=0), n, heads)
    d_qkv, fc_parts = after((d_qkv, fc_parts))

    grad_proj = rows_dot(mixed_low, d_branch).astype(BF).reshape(n, own_rows, D)
    proj_halves = after(core_halves(grad_proj), fc_parts)
    proj_part = reduce_rows([pick(proj_halves, me ^ d) for d in range(n)]).astype(BF)

    grad_main = rows_dot(normed, d_qkv[:, : 3 * main]).astype(BF).reshape(n, own_rows, 3 * main)
    grad_spare = rows_dot(normed, d_qkv[:, 3 * main :]).astype(BF).reshape(n, own_rows, 3 * spare)
    main_halves = core_halves(grad_main)
    spare_halves = core_halves(pick(grad_spare, me)[None])[0]
    attn_parts = jnp.concatenate(
        [pick(main_halves, me)]
        + [swap(pick(main_halves, me ^ d), d) for d in range(1, n)]
        + [spare_halves, proj_part],
        axis=1,
    )
    attn_sum = lax.psum(after(attn_parts, fc_sum), "plane")

    counted = (lax.broadcasted_iota(jnp.int32, (n * rows, 1), 0) < rows) | (
        lax.broadcasted_iota(jnp.int32, (1, d_qkv.shape[1]), 1) < 3 * main
    )
    d_once = after(jnp.where(counted, d_qkv, BF(0)), attn_parts)
    f = reduce_rows([cols_dot(block(d_once, d), w_attn) for d in range(n)])
    xhat_own, inv_own = normalize(own_tokens)
    f_gain = f * gain_one
    d_tokens = inv_own * (
        f_gain
        - jnp.mean(f_gain, axis=-1, keepdims=True)
        - xhat_own * jnp.mean(f_gain * xhat_own, axis=-1, keepdims=True)
    )
    input_grad = (d_middle + d_tokens).astype(BF)[None]

    late_active = after(active, attn_parts)
    out_parts = [
        jnp.dot(block(late_active, d), out_weight, preferred_element_type=F32) for d in range(n)
    ]
    output = (middle + reduce_rows(out_parts) + b_out).astype(BF)[None]

    sum_fc_weight = local_call(
        functools.partial(
            unpack_kernel,
            n,
            half,
            step,
            lambda m, d: [(0, (m ^ d) * own_ff, 0, d * half, 0, own_ff)],
            1,
        ),
        [jax.ShapeDtypeStruct((own_rows, n * own_ff), F32)],
        own_rows * n * own_ff * 8,
        at,
        fc_sum,
        swap_core(fc_sum),
    )[0]

    def attn_places(m, d):
        base = d * 3 * main
        places = [
            (0, p * D + (m ^ d) * main, 0, 0, base + p * main, base + (p + 1) * main)
            for p in range(3)
        ]
        if d == 0:
            base = n * 3 * main
            places += [
                (0, p * D + n * main, 0, 0, base + p * spare, base + (p + 1) * spare)
                for p in range(3)
            ]
            places.append((1, 0, 0, 0, 3 * D, 4 * D))
        return places

    d_once_sum = jnp.sum(d_once.astype(F32), axis=0)

    def vector_of(part):
        whole = jnp.zeros((D,), F32)
        whole = lax.dynamic_update_slice_in_dim(
            whole, d_once_sum[part * main : (part + 1) * main], me * main, 0
        )
        lane = 3 * main + part * spare
        return jnp.concatenate([whole[: n * main], d_once_sum[lane : lane + spare]])

    small_grads = jnp.stack(
        [
            vector_of(0),
            vector_of(2),
            jnp.sum(d_branch.astype(F32), axis=0),
            jnp.sum(f * xhat_own, axis=0),
            jnp.sum(f, axis=0),
            jnp.sum(e * xhat_two, axis=0),
            jnp.sum(e, axis=0),
            jnp.sum(own_cot.astype(F32), axis=0),
        ]
    )
    small_grads = small_grads.reshape(8, n, own_rows).transpose(1, 0, 2)
    small_own = pick(small_grads, me)
    for d in range(1, n):
        small_own = small_own + swap(pick(small_grads, me ^ d), d)
    small_own = jnp.concatenate([small_own, grad_fc_bias.reshape(-1, own_rows)], axis=0)
    small_own = small_own + swap_core(small_own)
    hop = 1
    while hop < planes:
        small_own = small_own + lax.ppermute(
            small_own, "plane", [(i, i ^ hop) for i in range(planes)]
        )
        hop *= 2
    sum_out_weight = sum_out_weight.astype(F32)
    attn_sum, small_own, output, input_grad, sum_fc_weight, sum_out_weight = after(
        (attn_sum, small_own, output, input_grad, sum_fc_weight, sum_out_weight)
    )
    sum_attn_weight, sum_proj_weight = local_call(
        functools.partial(unpack_kernel, n, half, step, attn_places, 1),
        [
            jax.ShapeDtypeStruct((own_rows, 3 * D), F32),
            jax.ShapeDtypeStruct((own_rows, D), F32),
        ],
        own_rows * 4 * D * 8,
        at,
        attn_sum,
        swap_core(attn_sum),
    )
    s = small_own[:8]
    sum_fc_bias = small_own[8:].reshape(-1)
    return (
        output,
        input_grad,
        sum_attn_weight,
        s[0],
        s[1],
        sum_proj_weight,
        s[2],
        s[3],
        s[4],
        s[5],
        s[6],
        sum_fc_weight,
        sum_fc_bias,
        sum_out_weight,
        s[7],
    )


def solution(mesh):
    shards, reps = mesh.devices.shape
    split = jax.sharding.Mesh(
        mesh.devices.reshape(shards, reps // 2, 2), ("shard", "plane", "core")
    )
    rep = ("plane", "core")
    batch = P(rep, "shard", None)
    row, vec = P("shard", None), P("shard")
    return jax.shard_map(
        body,
        mesh=split,
        in_specs=(batch, batch, P(rep, None), row, vec, vec, row)
        + (vec,) * 5
        + (row, vec, row, vec),
        out_specs=(batch, batch, row, vec, vec, row) + (vec,) * 5 + (row, vec, row, vec),
        check_vma=False,
    )
```

profile of v0, /device:TPU:0, one launch (start us, length us, event | category | flops | bytes accessed | tf_op | source)
XLA Modules:
  0.0 617.8 jit_solution(3634638782069391388)
XLA Ops:
  27.8 17.4 %collective-permute-done.refs_1_ = bf16[224,1344]{1,0:T(8,128)(2,1)S(1)} collective-permute-done((bf16[224,1344]{1,0:T(8,128)(2,1)}, bf16[224,1344]{1,0:T(8,128)(2,1)S(1)}, u32[]{:S(2)}, u32[]{:S(2)}) %collective-permute-start) | collective-permute-done | bytes 602144 | tf_op jit(solution)/shard_map/ppermute | solution.py:433
  45.2 11.8 %collective-permute-done.2.refs_3_ = bf16[224,1344]{1,0:T(8,128)(2,1)S(1)} collective-permute-done((bf16[224,1344]{1,0:T(8,128)(2,1)}, bf16[224,1344]{1,0:T(8,128)(2,1)S(1)}, u32[]{:S(2)}, u32[]{:S(2)}) %collective-permute-start.2) | collective-permute-done | bytes 602144 | tf_op jit(solution)/shard_map/ppermute | solution.py:433
  74.4 18.6 %collective-permute-done.5 = bf16[128,1600]{0,1:T(8,128)(2,1)S(1)} collective-permute-done((bf16[128,1600]{0,1:T(8,128)(2,1)}, bf16[128,1600]{0,1:T(8,128)(2,1)S(1)}, u32[]{:S(2)}, u32[]{:S(2)}) %collective-permute-start.5) | collective-permute-done | bytes 409632 | tf_op jit(solution)/shard_map/ppermute | solution.py:433
  100.7 9.3 %add_convert_fusion.qkv_ref = bf16[1024,1344]{1,0:T(8,128)(2,1)S(1)} fusion(bf16[1600,1344]{1,0:T(8,128)(2,1)} %get-tuple-element.94, f32[1344]{0:T(1024)S(1)} %concatenate.72, bf16[1024,1600]{0,1:T(8,128)(2,1)} %copy-done.23, f32[1600]{0:T(1024)S(1)} %get-tuple-element.165, f32[1600]{0:T(1024)S(1)} %get-tuple-element.166, f32[1024]{0:T(1024)S(1)} %add_rsqrt_fusion, ...), kind=kOutput, calls=%fused_computation.14 | convolution fusion | flops 4416602112 | bytes 10356480 | tf_op jit(solution)/shard_map/dot_general | solution.py:577
  118.3 13.1 %shard_map.274 = bf16[1024,448]{1,0:T(8,128)(2,1)S(1)} custom-call(s32[4]{0:T(128)S(1)} %pad_add_fusion.1.info_ref, bf16[1024,1344]{1,0:T(8,128)(2,1)S(1)} %add_convert_fusion.qkv_ref), custom_call_target="tpu_custom_call" | custom-call | flops 1 | bytes 1 | tf_op jit(solution)/shard_map/pallas_call | solution.py:200
  134.5 7.7 %collective-permute-done.14 = bf16[112,1600]{1,0:T(8,128)(2,1)S(1)} collective-permute-done((bf16[112,1600]{1,0:T(8,128)(2,1)}, bf16[112,1600]{1,0:T(8,128)(2,1)S(1)}, u32[]{:S(2)}, u32[]{:S(2)}) %collective-permute-start.14) | collective-permute-done | bytes 358432 | tf_op jit(solution)/shard_map/ppermute | solution.py:433
  171.6 7.7 %collective-permute-done.21.near = bf16[336,1600]{1,0:T(8,128)(2,1)S(1)} collective-permute-done((bf16[336,1600]{1,0:T(8,128)(2,1)S(1)}, bf16[336,1600]{1,0:T(8,128)(2,1)S(1)}, u32[]{:S(2)}, u32[]{:S(2)}) %collective-permute-start.21) | collective-permute-done | bytes 1075232 | tf_op jit(solution)/shard_map/ppermute | solution.py:436
  180.6 10.6 %convolution_convert_fusion.4 = bf16[1024,1600]{0,1:T(8,128)(2,1)} fusion(bf16[1600,1600]{1,0:T(8,128)(2,1)} %param.30, bf16[256,1600]{0,1:T(8,128)(2,1)S(1)} %get-tuple-element.176, bf16[256,1600]{0,1:T(8,128)(2,1)S(1)} %get-tuple-element.177, bf16[256,1600]{0,1:T(8,128)(2,1)S(1)} %get-tuple-element.175, bf16[256,1600]{0,1:T(8,128)(2,1)S(1)} %bitcast.163), kind=kOutput, calls=%fused_computation.19 | convolution fusion | flops 5257625600 | bytes 11673600 | tf_op jit(solution)/shard_map/dot_general | solution.py:23
  195.1 8.5 %collective-permute-done.23 = bf16[128,1600]{0,1:T(8,128)(2,1)S(1)} collective-permute-done((bf16[128,1600]{0,1:T(8,128)(2,1)S(1)}, bf16[128,1600]{0,1:T(8,128)(2,1)S(1)}, u32[]{:S(2)}, u32[]{:S(2)}) %collective-permute-start.23) | collective-permute-done | bytes 409632 | tf_op jit(solution)/shard_map/ppermute | solution.py:433
  226.3 9.0 %convolution_convert_fusion.2 = bf16[1600,1600]{1,0:T(8,128)(2,1)} fusion(bf16[256,1600]{0,1:T(8,128)(2,1)S(1)} %copy-done.50, bf16[256,1600]{0,1:T(8,128)(2,1)S(1)} %copy-done.52, bf16[256,1600]{0,1:T(8,128)(2,1)S(1)} %copy-done.48, bf16[256,1600]{0,1:T(8,128)(2,1)S(1)} %bitcast.164, bf16[256,1600]{0,1:T(8,128)(2,1)S(1)} %get-tuple-element.225, ...), kind=kOutput, calls=%fused_computation.6 | convolution fusion | flops 5271654400 | bytes 11673600 | tf_op jit(solution)/shard_map/dot_general | solution.py:23
  235.4 6.5 %multiply_convert_fusion = (bf16[256,1600]{0,1:T(8,128)(2,1)S(1)}, bf16[256,1600]{0,1:T(8,128)(2,1)S(1)}, bf16[256,1600]{0,1:T(8,128)(2,1)S(1)}, bf16[256,1600]{0,1:T(8,128)(2,1)S(1)}) fusion(f32[256,1600]{0,1:T(8,128)} %get-tuple-element.226, bf16[1024,1600]{0,1:T(8,128)(2,1)} %convolution_convert_fusion.4, f32[256,1600]{0,1:T(8,128)S(1)} %get-tuple-element.228, ...), kind=kLoop, calls=%fused_computation.107 | loop fusion | flops 36044800 | bytes 13107200 | tf_op jit(solution)/shard_map/convert_element_type | solution.py:636
  255.8 11.1 %convolution_convert_fusion.1 = bf16[1600,1600]{1,0:T(8,128)(2,1)} fusion(bf16[1024,1600]{0,1:T(8,128)(2,1)} %constant_dynamic-update-slice_fusion.8, bf16[256,1600]{0,1:T(8,128)(2,1)S(1)} %get-tuple-element.171, bf16[256,1600]{0,1:T(8,128)(2,1)S(1)} %get-tuple-element.172, bf16[256,1600]{0,1:T(8,128)(2,1)S(1)} %get-tuple-element.173, ...), kind=kOutput, calls=%fused_computation.5 | convolution fusion | flops 5258547200 | bytes 11673600 | tf_op jit(solution)/shard_map/dot_general | solution.py:23
  273.7 17.2 %collective-permute-done.26 = bf16[256,1600]{0,1:T(8,128)(2,1)S(1)} collective-permute-done((bf16[256,1600]{0,1:T(8,128)(2,1)}, bf16[256,1600]{0,1:T(8,128)(2,1)S(1)}, u32[]{:S(2)}, u32[]{:S(2)}) %collective-permute-start.26) | collective-permute-done | bytes 819232 | tf_op jit(solution)/shard_map/ppermute | solution.py:433
  332.2 27.9 %shard_map.277 = bf16[1024,1344]{1,0:T(8,128)(2,1)S(1)} custom-call(s32[4]{0:T(128)S(1)} %pad_add_fusion.1.info_ref, bf16[1024,1344]{1,0:T(8,128)(2,1)} %copy-done, bf16[1024,448]{1,0:T(8,128)(2,1)S(1)} %copy-done.1), custom_call_target="tpu_custom_call" | custom-call | flops 1 | bytes 1 | tf_op jit(solution)/shard_map/pallas_call | solution.py:200
  360.1 7.4 %convert_element_type.311 = f32[1600,1600]{1,0:T(8,128)} convert(bf16[1600,1600]{1,0:T(8,128)(2,1)} %all-reduce.8.cloned.1.call-done) | non-fusion elementwise | flops 2560000 | bytes 15360000 | tf_op jit(solution)/shard_map/convert_element_type | solution.py:767
  371.6 6.8 %convolution_convert_fusion = bf16[1600,1152]{1,0:T(8,128)(2,1)S(1)} fusion(bf16[1024,1344]{1,0:T(8,128)(2,1)S(1)} %shard_map.277, bf16[1024,1600]{0,1:T(8,128)(2,1)} %copy-done.23, f32[1600]{0:T(1024)S(1)} %copy-done.71, f32[1600]{0:T(1024)S(1)} %copy-done.60, f32[1024]{0:T(1024)S(1)} %copy-done.76, f32[1024]{0:T(1024)S(1)} %copy-done.67), kind=kOutput, calls=%fused_computation.4 | convolution fusion | flops 3786547200 | bytes 9347072 | tf_op jit(solution)/shard_map/dot_general | solution.py:23
  397.0 12.3 %collective-permute-done.43 = bf16[208,1600]{1,0:T(8,128)(2,1)S(1)} collective-permute-done((bf16[208,1600]{1,0:T(8,128)(2,1)S(1)}, bf16[208,1600]{1,0:T(8,128)(2,1)S(1)}, u32[]{:S(2)}, u32[]{:S(2)}) %collective-permute-start.43) | collective-permute-done | bytes 665632 | tf_op jit(solution)/shard_map/ppermute | solution.py:433
  409.3 14.1 %collective-permute-done.42 = bf16[208,1600]{1,0:T(8,128)(2,1)S(1)} collective-permute-done((bf16[208,1600]{1,0:T(8,128)(2,1)S(1)}, bf16[208,1600]{1,0:T(8,128)(2,1)S(1)}, u32[]{:S(2)}, u32[]{:S(2)}) %collective-permute-start.42) | collective-permute-done | bytes 665632 | tf_op jit(solution)/shard_map/ppermute | solution.py:433
  429.6 10.9 %collective-permute-done.38 = bf16[208,1152]{1,0:T(8,128)(2,1)S(1)} collective-permute-done((bf16[208,1152]{1,0:T(8,128)(2,1)S(1)}, bf16[208,1152]{1,0:T(8,128)(2,1)S(1)}, u32[]{:S(2)}, u32[]{:S(2)}) %collective-permute-start.38) | collective-permute-done | bytes 479264 | tf_op jit(solution)/shard_map/ppermute | solution.py:433
  440.5 9.2 %collective-permute-done.37 = bf16[208,1152]{1,0:T(8,128)(2,1)S(1)} collective-permute-done((bf16[208,1152]{1,0:T(8,128)(2,1)S(1)}, bf16[208,1152]{1,0:T(8,128)(2,1)S(1)}, u32[]{:S(2)}, u32[]{:S(2)}) %collective-permute-start.37) | collective-permute-done | bytes 479264 | tf_op jit(solution)/shard_map/ppermute | solution.py:433
  490.8 14.6 %collective-permute-done.44 = bf16[256,1600]{0,1:T(8,128)(2,1)} collective-permute-done((bf16[256,1600]{0,1:T(8,128)(2,1)}, bf16[256,1600]{0,1:T(8,128)(2,1)}, u32[]{:S(2)}, u32[]{:S(2)}) %collective-permute-start.44) | collective-permute-done | bytes 819232 | tf_op jit(solution)/shard_map/ppermute | solution.py:433
  506.9 33.8 %collective-permute-done.45 = bf16[256,1600]{0,1:T(8,128)(2,1)} collective-permute-done((bf16[256,1600]{0,1:T(8,128)(2,1)}, bf16[256,1600]{0,1:T(8,128)(2,1)}, u32[]{:S(2)}, u32[]{:S(2)}) %collective-permute-start.45) | collective-permute-done | bytes 819232 | tf_op jit(solution)/shard_map/ppermute | solution.py:433
  540.8 6.6 %fusion.18 = (f32[256]{0:T(256)S(1)}, f32[1600]{0:T(1024)S(1)}, f32[256]{0:T(256)S(1)}, f32[1600]{0:T(1024)S(1)}, f32[256,1600]{0,1:T(8,128)}) fusion(f32[1600]{0:T(1024)S(1)} %copy-done.60, f32[256]{0:T(256)S(1)} %copy-done.78, f32[256]{0:T(256)S(1)} %copy-done.69, bf16[1,256,1600]{1,2,0:T(8,128)(2,1)} %param.16, ...), kind=kOutput, calls=%fused_computation.69 | convolution fusion | flops 1107554816 | bytes 10164992 | tf_op jit(solution)/shard_map/dot_general | solution.py:23
  574.9 23.1 %all-reduce.6.cloned.1.call-done.refs_0_ = bf16[208,6400]{1,0:T(8,128)(2,1)} async-done(((bf16[208,6400]{1,0:T(8,128)(2,1)}), bf16[208,6400]{1,0:T(8,128)(2,1)}) %all-reduce.6.cloned.1.call-update) | async-done | bytes 2662416 | tf_op jit(solution)/shard_map/psum | solution.py:680
  (452 shorter events, 287.0 us)
Async XLA Ops:
  7.2 152.9 %all-gather.2.cloned.1.call-start = ((), (), s32[]{:S(2)}) async-start(), calls=%async_computation | async-start | bytes 4096000 | tf_op jit(solution)/shard_map/all_gather | solution.py:557
  7.2 49.8 %collective-permute-start.4 = (bf16[256,1600]{0,1:T(8,128)(2,1)}, bf16[256,1600]{0,1:T(8,128)(2,1)}, u32[]{:S(2)}, u32[]{:S(2)}) collective-permute-start(bf16[256,1600]{0,1:T(8,128)(2,1)} %bitcast.150), channel_id=1, source_target_pairs={{0,16},{8,24},{16,0},{24,8},{1,17},{9,25},{17,1},{25,9},{2,18},{10... | collective-permute-start | bytes 2457608 | tf_op jit(solution)/shard_map/ppermute | solution.py:433
  10.3 46.8 %collective-permute-start.3 = (bf16[256,1600]{0,1:T(8,128)(2,1)}, bf16[256,1600]{0,1:T(8,128)(2,1)}, u32[]{:S(2)}, u32[]{:S(2)}) collective-permute-start(bf16[256,1600]{0,1:T(8,128)(2,1)} %bitcast.151), channel_id=1, source_target_pairs={{0,8},{8,0},{16,24},{24,16},{1,9},{9,1},{17,25},{25,17},{2,10},{10... | collective-permute-start | bytes 2457608 | tf_op jit(solution)/shard_map/ppermute | solution.py:433
  22.8 34.2 %collective-permute-start.2 = (bf16[224,1344]{1,0:T(8,128)(2,1)}, bf16[224,1344]{1,0:T(8,128)(2,1)S(1)}, u32[]{:S(2)}, u32[]{:S(2)}) collective-permute-start(bf16[224,1344]{1,0:T(8,128)(2,1)} %get-tuple-element.86), channel_id=1, source_target_pairs={{0,24},{8,16},{16,8},{24,0},{1,25},{9,17},{17,9},{25,1},{2,26},{10... | collective-permute-start | bytes 1806344 | tf_op jit(solution)/shard_map/ppermute | solution.py:433
  58.8 51.3 %collective-permute-start.9 = (bf16[208,1600]{1,0:T(8,128)(2,1)}, bf16[208,1600]{1,0:T(8,128)(2,1)}, u32[]{:S(2)}, u32[]{:S(2)}) collective-permute-start(bf16[208,1600]{1,0:T(8,128)(2,1)} %constant_dynamic-slice_fusion.11), channel_id=1, source_target_pairs={{0,16},{8,24},{16,0},{24,8},{1,17},{9,25},{17,1},{25,9},{2,18},{10... | collective-permute-start | bytes 1996808 | tf_op jit(solution)/shard_map/ppermute | solution.py:433
  60.4 49.7 %collective-permute-start.8 = (bf16[208,1600]{1,0:T(8,128)(2,1)}, bf16[208,1600]{1,0:T(8,128)(2,1)}, u32[]{:S(2)}, u32[]{:S(2)}) collective-permute-start(bf16[208,1600]{1,0:T(8,128)(2,1)} %constant_dynamic-slice_fusion.11), channel_id=1, source_target_pairs={{0,8},{8,0},{16,24},{24,16},{1,9},{9,1},{17,25},{25,17},{2,10},{10... | collective-permute-start | bytes 1996808 | tf_op jit(solution)/shard_map/ppermute | solution.py:433
  64.9 295.2 %all-reduce.8.cloned.1.call-start = ((), (), s32[]{:S(2)}) async-start(), calls=%async_computation.3 | async-start | bytes 10649600 | tf_op jit(solution)/shard_map/psum | solution.py:633
  235.3 255.5 %all-reduce.4.cloned.1.call-start = ((), (), s32[]{:S(2)}) async-start(), calls=%async_computation.1 | async-start | bytes 5537792 | tf_op jit(solution)/shard_map/psum | solution.py:660
  253.8 37.1 %collective-permute-start.26 = (bf16[256,1600]{0,1:T(8,128)(2,1)}, bf16[256,1600]{0,1:T(8,128)(2,1)S(1)}, u32[]{:S(2)}, u32[]{:S(2)}) collective-permute-start(bf16[256,1600]{0,1:T(8,128)(2,1)} %convolution_convert_fusion.9), channel_id=1, source_target_pairs={{0,16},{8,24},{16,0},{24,8},{1,17},{9,25},{17,1},{25,9},{2,18},{10... | collective-permute-start | bytes 2457608 | tf_op jit(solution)/shard_map/ppermute | solution.py:433
  254.4 36.5 %collective-permute-start.27 = (bf16[256,1600]{0,1:T(8,128)(2,1)}, bf16[256,1600]{0,1:T(8,128)(2,1)}, u32[]{:S(2)}, u32[]{:S(2)}) collective-permute-start(bf16[256,1600]{0,1:T(8,128)(2,1)} %convolution_convert_fusion.8), channel_id=1, source_target_pairs={{0,24},{8,16},{16,8},{24,0},{1,25},{9,17},{17,9},{25,1},{2,26},{10... | collective-permute-start | bytes 2457608 | tf_op jit(solution)/shard_map/ppermute | solution.py:433
  271.5 34.6 %collective-permute-start.31 = (bf16[4,208,1600]{2,1,0:T(8,128)(2,1)S(1)}, bf16[4,208,1600]{2,1,0:T(8,128)(2,1)S(1)}, u32[]{:S(2)}, u32[]{:S(2)}) collective-permute-start(bf16[4,208,1600]{2,1,0:T(8,128)(2,1)S(1)} %constant_dynamic-slice_fusion.7), channel_id=1, source_target_pairs={{0,1},{1,0},{2,3},{3,2},{4,5},{5,4},{6,7},{7,6},{8,9},{9,8},{10,11... | collective-permute-start | bytes 7987208 | tf_op jit(solution)/shard_map/ppermute | solution.py:439
  315.8 51.8 %collective-permute-start.34 = (bf16[208,1600]{1,0:T(8,128)(2,1)}, bf16[208,1600]{1,0:T(8,128)(2,1)}, u32[]{:S(2)}, u32[]{:S(2)}) collective-permute-start(bf16[208,1600]{1,0:T(8,128)(2,1)} %get-tuple-element.182), channel_id=1, source_target_pairs={{0,24},{8,16},{16,8},{24,0},{1,25},{9,17},{17,9},{25,1},{2,26},{10... | collective-permute-start | bytes 1996808 | tf_op jit(solution)/shard_map/ppermute | solution.py:433
  316.9 50.6 %collective-permute-start.33 = (bf16[208,1600]{1,0:T(8,128)(2,1)}, bf16[208,1600]{1,0:T(8,128)(2,1)}, u32[]{:S(2)}, u32[]{:S(2)}) collective-permute-start(bf16[208,1600]{1,0:T(8,128)(2,1)} %get-tuple-element.183), channel_id=1, source_target_pairs={{0,16},{8,24},{16,0},{24,8},{1,17},{9,25},{17,1},{25,9},{2,18},{10... | collective-permute-start | bytes 1996808 | tf_op jit(solution)/shard_map/ppermute | solution.py:433
  318.1 49.5 %collective-permute-start.32 = (bf16[208,1600]{1,0:T(8,128)(2,1)}, bf16[208,1600]{1,0:T(8,128)(2,1)}, u32[]{:S(2)}, u32[]{:S(2)}) collective-permute-start(bf16[208,1600]{1,0:T(8,128)(2,1)} %get-tuple-element.184), channel_id=1, source_target_pairs={{0,8},{8,0},{16,24},{24,16},{1,9},{9,1},{17,25},{25,17},{2,10},{10... | collective-permute-start | bytes 1996808 | tf_op jit(solution)/shard_map/ppermute | solution.py:433
  321.0 65.3 %collective-permute-start.40 = (bf16[4,208,1600]{2,1,0:T(8,128)(2,1)}, bf16[4,208,1600]{2,1,0:T(8,128)(2,1)}, u32[]{:S(2)}, u32[]{:S(2)}) collective-permute-start(bf16[4,208,1600]{2,1,0:T(8,128)(2,1)} %constant_dynamic-slice_fusion.4), channel_id=1, source_target_pairs={{0,1},{1,0},{2,3},{3,2},{4,5},{5,4},{6,7},{7,6},{8,9},{9,8},{10,11... | collective-permute-start | bytes 7987208 | tf_op jit(solution)/shard_map/ppermute | solution.py:439
  370.9 227.1 %all-reduce.6.cloned.1.call-start = ((), (), s32[]{:S(2)}) async-start(), calls=%async_computation.2 | async-start | bytes 5324800 | tf_op jit(solution)/shard_map/psum | solution.py:680
  381.7 41.8 %collective-permute-start.35 = (bf16[4,208,1152]{2,1,0:T(8,128)(2,1)}, bf16[4,208,1152]{2,1,0:T(8,128)(2,1)}, u32[]{:S(2)}, u32[]{:S(2)}) collective-permute-start(bf16[4,208,1152]{2,1,0:T(8,128)(2,1)} %constant_dynamic-slice_fusion.6), channel_id=1, source_target_pairs={{0,1},{1,0},{2,3},{3,2},{4,5},{5,4},{6,7},{7,6},{8,9},{9,8},{10,11... | collective-permute-start | bytes 5750792 | tf_op jit(solution)/shard_map/ppermute | solution.py:439
  391.0 32.5 %collective-permute-start.42 = (bf16[208,1600]{1,0:T(8,128)(2,1)S(1)}, bf16[208,1600]{1,0:T(8,128)(2,1)S(1)}, u32[]{:S(2)}, u32[]{:S(2)}) collective-permute-start(bf16[208,1600]{1,0:T(8,128)(2,1)S(1)} %get-tuple-element.179), channel_id=1, source_target_pairs={{0,16},{8,24},{16,0},{24,8},{1,17},{9,25},{17,1},{25,9},{2,18},{10... | collective-permute-start | bytes 1996808 | tf_op jit(solution)/shard_map/ppermute | solution.py:433
  466.5 81.1 %collective-permute-start.53 = (bf16[256,1600]{0,1:T(8,128)(2,1)}, bf16[256,1600]{0,1:T(8,128)(2,1)}, u32[]{:S(2)}, u32[]{:S(2)}) collective-permute-start(bf16[256,1600]{0,1:T(8,128)(2,1)} %convolution_convert_fusion.13), channel_id=1, source_target_pairs={{0,8},{8,0},{16,24},{24,16},{1,9},{9,1},{17,25},{25,17},{2,10},{10... | collective-permute-start | bytes 2457608 | tf_op jit(solution)/shard_map/ppermute | solution.py:433
  467.8 79.8 %collective-permute-start.54 = (bf16[256,1600]{0,1:T(8,128)(2,1)}, bf16[256,1600]{0,1:T(8,128)(2,1)}, u32[]{:S(2)}, u32[]{:S(2)}) collective-permute-start(bf16[256,1600]{0,1:T(8,128)(2,1)} %convolution_convert_fusion.12), channel_id=1, source_target_pairs={{0,16},{8,24},{16,0},{24,8},{1,17},{9,25},{17,1},{25,9},{2,18},{10... | collective-permute-start | bytes 2457608 | tf_op jit(solution)/shard_map/ppermute | solution.py:433
  473.3 32.2 %collective-permute-start.44 = (bf16[256,1600]{0,1:T(8,128)(2,1)}, bf16[256,1600]{0,1:T(8,128)(2,1)}, u32[]{:S(2)}, u32[]{:S(2)}) collective-permute-start(bf16[256,1600]{0,1:T(8,128)(2,1)} %convolution_convert_fusion.7), channel_id=1, source_target_pairs={{0,8},{8,0},{16,24},{24,16},{1,9},{9,1},{17,25},{25,17},{2,10},{10... | collective-permute-start | bytes 2457608 | tf_op jit(solution)/shard_map/ppermute | solution.py:433
  479.4 61.3 %collective-permute-start.45 = (bf16[256,1600]{0,1:T(8,128)(2,1)}, bf16[256,1600]{0,1:T(8,128)(2,1)}, u32[]{:S(2)}, u32[]{:S(2)}) collective-permute-start(bf16[256,1600]{0,1:T(8,128)(2,1)} %convolution_convert_fusion.6), channel_id=1, source_target_pairs={{0,16},{8,24},{16,0},{24,8},{1,17},{9,25},{17,1},{25,9},{2,18},{10... | collective-permute-start | bytes 2457608 | tf_op jit(solution)/shard_map/ppermute | solution.py:433
  482.6 58.1 %collective-permute-start.46 = (bf16[256,1600]{0,1:T(8,128)(2,1)}, bf16[256,1600]{0,1:T(8,128)(2,1)}, u32[]{:S(2)}, u32[]{:S(2)}) collective-permute-start(bf16[256,1600]{0,1:T(8,128)(2,1)} %convolution_convert_fusion.5), channel_id=1, source_target_pairs={{0,24},{8,16},{16,8},{24,0},{1,25},{9,17},{17,9},{25,1},{2,26},{10... | collective-permute-start | bytes 2457608 | tf_op jit(solution)/shard_map/ppermute | solution.py:433
  505.5 42.1 %collective-permute-start.55 = (bf16[256,1600]{0,1:T(8,128)(2,1)}, bf16[256,1600]{0,1:T(8,128)(2,1)}, u32[]{:S(2)}, u32[]{:S(2)}) collective-permute-start(bf16[256,1600]{0,1:T(8,128)(2,1)} %convolution_convert_fusion.11), channel_id=1, source_target_pairs={{0,24},{8,16},{16,8},{24,0},{1,25},{9,17},{17,9},{25,1},{2,26},{10... | collective-permute-start | bytes 2457608 | tf_op jit(solution)/shard_map/ppermute | solution.py:433
  (129 other events, 1578.9 us)
Sparse Core Ops, SparseCore 0:
  65.0 57.4 all-gather.1
  235.4 118.4 all-reduce.7
  371.0 108.6 all-reduce.3
  490.9 106.9 all-reduce.5
where the time goes:
time: 628 us; the launch traced here: 618 us
  waiting for transfers between devices  233 us (37%)
  matrix products  128 us (20%)
  Pallas kernels  72.4 us (12%)
  starting transfers between devices  59.8 us (10%)
  local copies, waits for them, and re-layouts  56.5 us (9%)
  other arithmetic  53 us (8%)
  between operations  15.5 us (2%)
    ppermute x45, waiting for transfers between devices, swap(): return lax.ppermute(value, 'shard', [(i, i ^ d) for i in range(n)])  190 us
    dot_general x15, matrix products, dot(): lax.dot_general(left, right, (dims, ((), ())), preferred_element_type=F32)  77.8 us
    ppermute x45, starting transfers between devices, swap(): return lax.ppermute(value, 'shard', [(i, i ^ d) for i in range(n)])  53.4 us
    pallas_call x2, Pallas kernels, vmem_call(): pl.pallas_call(kernel, out_shape=out_shape, in_specs=[pl.BlockSpec(memory...  41 us
    pallas_call x7, Pallas kernels, local_call(): pl.pallas_call(kernel, out_shape=out_shape, in_specs=[pl.BlockSpec(memory...  31.4 us
    unnamed x205, local copies, waits for them, and re-layouts  25.9 us
    psum x1, waiting for transfers between devices, body(): attn_sum = lax.psum(after(attn_parts, fc_sum), 'plane')  23.1 us
    dot_general x4, matrix products, body(): jnp.dot(block(late_active, d), out_weight, preferred_element_type=F32)  18.7 us
  transfers between devices with their start and end apart: 62, of which 24 were waited for; matrix products, arithmetic and copies ran while one was open for 31% of the time, Pallas kernels for 10%

commit v1 on v0

--- a/solution.py
+++ b/solution.py
@@ -580,7 +580,8 @@
     fc_got = [swap(fc_sent[d], d) for d in range(1, n)]
     info = jnp.concatenate([lengths[0], me.astype(jnp.int32)[None]])
     mixed_heads = attention_fwd(info, qkv, n, heads)
-    mixed_heads, proj_parts, fc_got = after((mixed_heads, proj_parts, fc_got))
+    mixed_heads, proj_parts, fc_first = after((mixed_heads, proj_parts, fc_got[:-1]))
+    fc_got = list(fc_first) + fc_got[-1:]
     if by_parts:
         fc_mine = jnp.concatenate(fc_got)
         fc_near = swap_plane(fc_mine)
@@ -595,7 +596,13 @@
     xhat_two, inv_two = normalize(middle)
     own_normed_two = (xhat_two * gain_two + bias_two).astype(BF)
     normed_near = gather_near(own_normed_two)
+    cot_parts = [own_cot] + [
+        lax.dynamic_slice_in_dim(cot_all, (me ^ d) * rows, rows, 0) for d in range(1, n)
+    ]
+    group_cot = jnp.concatenate(cot_parts, axis=0)
+    d_active = cols_dot(group_cot, out_weight).astype(BF)
     if by_parts:
+        fc_mine, fc_near, d_active = after((fc_mine, fc_near, d_active), own_normed_two)
         w_fc = local_call(
             functools.partial(place_part_kernel, n, length, stride, own_rows),
             jax.ShapeDtypeStruct((D, own_ff), BF),
@@ -604,18 +611,11 @@
             fc_sent[0],
             fc_mine,
             fc_near,
-            swap_core(jnp.concatenate(after([fc_mine, fc_near], own_normed_two))),
+            swap_core(jnp.concatenate([fc_mine, fc_near])),
         )
     else:
         w_fc = place(fc_sent[0], fc_got)
-    cot_parts = [own_cot] + [
-        lax.dynamic_slice_in_dim(cot_all, (me ^ d) * rows, rows, 0) for d in range(1, n)
-    ]
-    group_cot = jnp.concatenate(cot_parts, axis=0)
-    d_active = cols_dot(group_cot, out_weight).astype(BF)
     normed_near, d_active = after((normed_near, d_active))
-    normed_parts = gather_far(own_normed_two, normed_near)
-    normed_two = jnp.concatenate(normed_parts, axis=0)
 
     def feed(part):
         hidden = jnp.dot(part, w_fc, preferred_element_type=F32) + fc_bias.astype(F32)
@@ -625,7 +625,18 @@
         )
         return (0.5 * hidden * (1.0 + inner)).astype(BF), slope.astype(BF)
 
-    fed = [feed(part) for part in normed_parts]
+    if n == 4:
+        one, two = normed_near
+        cut = rows // 32 * 16
+        far = [swap(one[:cut], 2), swap(two[cut:], 1)]
+        fed = [feed(part) for part in (own_normed_two, one, two)]
+        far, fed = after((far, fed))
+        normed_parts = [own_normed_two, one, two, jnp.concatenate(far, axis=0)]
+        fed.append(feed(normed_parts[3]))
+    else:
+        normed_parts = gather_far(own_normed_two, normed_near)
+        fed = [feed(part) for part in normed_parts]
+    normed_two = jnp.concatenate(normed_parts, axis=0)
     active_parts = [a for a, _ in fed]
     active = jnp.concatenate(active_parts, axis=0)
 
@@ -658,6 +669,7 @@
         [pick(fc_halves, me)] + [swap(pick(fc_halves, me ^ d), d) for d in range(1, n)]
     )
     fc_sum = lax.psum(fc_parts, "plane")
+    sum_out_weight = after(sum_out_weight, fc_parts).astype(F32)
     grad_fc_bias = jnp.sum(d_hidden.astype(F32), axis=0)
 
     d_qkv = attention_bwd(info, qkv, jnp.concatenate(dmix_parts, axis=0), n, heads)
@@ -740,16 +752,25 @@
         lane = 3 * main + part * spare
         return jnp.concatenate([whole[: n * main], d_once_sum[lane : lane + spare]])
 
+    early = after(
+        (
+            jnp.sum(d_branch.astype(F32), axis=0),
+            jnp.sum(e * xhat_two, axis=0),
+            jnp.sum(e, axis=0),
+            jnp.sum(own_cot.astype(F32), axis=0),
+        ),
+        attn_parts,
+    )
     small_grads = jnp.stack(
         [
             vector_of(0),
             vector_of(2),
-            jnp.sum(d_branch.astype(F32), axis=0),
+            early[0],
             jnp.sum(f * xhat_own, axis=0),
             jnp.sum(f, axis=0),
-            jnp.sum(e * xhat_two, axis=0),
-            jnp.sum(e, axis=0),
-            jnp.sum(own_cot.astype(F32), axis=0),
+            early[1],
+            early[2],
+            early[3],
         ]
     )
     small_grads = small_grads.reshape(8, n, own_rows).transpose(1, 0, 2)
@@ -764,7 +785,6 @@
             small_own, "plane", [(i, i ^ hop) for i in range(planes)]
         )
         hop *= 2
-    sum_out_weight = sum_out_weight.astype(F32)
     attn_sum, small_own, output, input_grad, sum_fc_weight, sum_out_weight = after(
         (attn_sum, small_own, output, input_grad, sum_fc_weight, sum_out_weight)
     )

time: 628 us -> 627 us (level)
    ppermute x1, waiting for transfers between devices: 7.7 us -> 0.01 us  [swap_plane(): return lax.ppermute(value, 'plane', [(i, i ^ 1) for i in range(planes)])]
    ppermute x45, waiting for transfers between devices: 190 us -> 196 us  [swap(): return lax.ppermute(value, 'shard', [(i, i ^ d) for i in range(n)])]
    unnamed x205 -> x193, local copies, waits for them, and re-layouts: 25.9 us -> 27.8 us
  transfers between devices with their start and end apart: 62 -> 62, of which waited for: 24 -> 26; matrix products, arithmetic and copies ran while one was open for 31% -> 32% of each run, Pallas kernels for 10% -> 11%
where the time goes in v1:
time: 627 us; the launch traced here: 617 us
  waiting for transfers between devices  239 us (38%)
  matrix products  129 us (21%)
  Pallas kernels  75.4 us (12%)
  starting transfers between devices  56.5 us (9%)
  local copies, waits for them, and re-layouts  54.1 us (9%)
  other arithmetic  48.5 us (8%)
  between operations  15.6 us (2%)
    ppermute x45, waiting for transfers between devices, swap(): return lax.ppermute(value, 'shard', [(i, i ^ d) for i in range(n)])  196 us
    dot_general x15, matrix products, dot(): lax.dot_general(left, right, (dims, ((), ())), preferred_element_type=F32)  74.5 us
    ppermute x45, starting transfers between devices, swap(): return lax.ppermute(value, 'shard', [(i, i ^ d) for i in range(n)])  52.4 us
    pallas_call x2, Pallas kernels, vmem_call(): pl.pallas_call(kernel, out_shape=out_shape, in_specs=[pl.BlockSpec(memory...  43.4 us
    pallas_call x7, Pallas kernels, local_call(): pl.pallas_call(kernel, out_shape=out_shape, in_specs=[pl.BlockSpec(memory...  32 us
    unnamed x193, local copies, waits for them, and re-layouts  27.8 us
    psum x1, waiting for transfers between devices, body(): attn_sum = lax.psum(after(attn_parts, fc_sum), 'plane')  26.4 us
    dot_general x4, matrix products, feed(): jnp.dot(part, w_fc, preferred_element_type=F32) + fc_bias.astype(F32)  20.6 us
  transfers between devices with their start and end apart: 62, of which 26 were waited for; matrix products, arithmetic and copies ran while one was open for 32% of the time, Pallas kernels for 11%

profile of v1, /device:TPU:0, one launch (start us, length us, event | category | flops | bytes accessed | tf_op | source)
XLA Modules:
  0.0 617.4 jit_solution(16252117055633817756)
XLA Ops:
  27.9 17.3 %collective-permute-done.refs_1_ = bf16[224,1344]{1,0:T(8,128)(2,1)S(1)} collective-permute-done((bf16[224,1344]{1,0:T(8,128)(2,1)}, bf16[224,1344]{1,0:T(8,128)(2,1)S(1)}, u32[]{:S(2)}, u32[]{:S(2)}) %collective-permute-start) | collective-permute-done | bytes 602144 | tf_op jit(solution)/shard_map/ppermute | solution.py:433
  45.2 11.8 %collective-permute-done.2.refs_3_ = bf16[224,1344]{1,0:T(8,128)(2,1)S(1)} collective-permute-done((bf16[224,1344]{1,0:T(8,128)(2,1)}, bf16[224,1344]{1,0:T(8,128)(2,1)S(1)}, u32[]{:S(2)}, u32[]{:S(2)}) %collective-permute-start.2) | collective-permute-done | bytes 602144 | tf_op jit(solution)/shard_map/ppermute | solution.py:433
  74.4 18.5 %collective-permute-done.5 = bf16[128,1600]{0,1:T(8,128)(2,1)S(1)} collective-permute-done((bf16[128,1600]{0,1:T(8,128)(2,1)}, bf16[128,1600]{0,1:T(8,128)(2,1)S(1)}, u32[]{:S(2)}, u32[]{:S(2)}) %collective-permute-start.5) | collective-permute-done | bytes 409632 | tf_op jit(solution)/shard_map/ppermute | solution.py:433
  100.5 9.4 %add_convert_fusion.qkv_ref = bf16[1024,1344]{1,0:T(8,128)(2,1)S(1)} fusion(bf16[1600,1344]{1,0:T(8,128)(2,1)} %get-tuple-element.107, f32[1344]{0:T(1024)S(1)} %concatenate.72, bf16[1024,1600]{0,1:T(8,128)(2,1)} %copy-done.25, f32[1600]{0:T(1024)S(1)} %get-tuple-element.191, f32[1600]{0:T(1024)S(1)} %get-tuple-element.192, f32[1024]{0:T(1024)S(1)} %add_rsqrt_fusion, ...), kind=kOutput, calls=%fused_computation.14 | convolution fusion | flops 4416602112 | bytes 10356480 | tf_op jit(solution)/shard_map/dot_general | solution.py:577
  116.5 14.2 %shard_map.274 = bf16[1024,448]{1,0:T(8,128)(2,1)S(1)} custom-call(s32[4]{0:T(128)S(1)} %pad_add_fusion.1.info_ref, bf16[1024,1344]{1,0:T(8,128)(2,1)S(1)} %add_convert_fusion.qkv_ref), custom_call_target="tpu_custom_call" | custom-call | flops 1 | bytes 1 | tf_op jit(solution)/shard_map/pallas_call | solution.py:200
  141.4 7.3 %collective-permute-done.20 = bf16[112,1600]{1,0:T(8,128)(2,1)S(1)} collective-permute-done((bf16[112,1600]{1,0:T(8,128)(2,1)S(1)}, bf16[112,1600]{1,0:T(8,128)(2,1)S(1)}, u32[]{:S(2)}, u32[]{:S(2)}) %collective-permute-start.20) | collective-permute-done | bytes 358432 | tf_op jit(solution)/shard_map/ppermute | solution.py:433
  166.4 16.4 %convolution_convert_fusion.4 = bf16[1024,1600]{0,1:T(8,128)(2,1)} fusion(bf16[1600,1600]{1,0:T(8,128)(2,1)S(1)} %bitcast.183, bf16[256,1600]{0,1:T(8,128)(2,1)S(1)} %get-tuple-element.202, bf16[256,1600]{0,1:T(8,128)(2,1)S(1)} %get-tuple-element.203, bf16[256,1600]{0,1:T(8,128)(2,1)S(1)} %get-tuple-element.201, bf16[256,1600]{0,1:T(8,128)(2,1)S(1)} %bitcast.163), kind=kOutput, calls=%fused_computation.19 | convolution fusion | flops 5257625600 | bytes 11673600 | tf_op jit(solution)/shard_map/dot_general | solution.py:23
  190.7 17.3 %collective-permute-done.19 = bf16[256,1600]{0,1:T(8,128)(2,1)} collective-permute-done((bf16[256,1600]{0,1:T(8,128)(2,1)}, bf16[256,1600]{0,1:T(8,128)(2,1)}, u32[]{:S(2)}, u32[]{:S(2)}) %collective-permute-start.19) | collective-permute-done | bytes 819232 | tf_op jit(solution)/shard_map/ppermute | solution.py:433
  221.1 7.0 %fusion.44 = (bf16[256,1600]{0,1:T(8,128)(2,1)}, bf16[256,1600]{0,1:T(8,128)(2,1)S(1)}) fusion(f32[1600]{0:T(1024)S(1)} %convert_element_type.242, bf16[256,1600]{0,1:T(8,128)(2,1)} %collective-permute-done.19, bf16[1600,1600]{1,0:T(8,128)(2,1)} %shard_map.276), kind=kOutput, calls=%fused_computation.95 | convolution fusion | flops 1319321600 | bytes 7584000 | tf_op jit(solution)/shard_map/dot_general | solution.py:621
  243.7 8.7 %convolution_convert_fusion.2 = bf16[1600,1600]{1,0:T(8,128)(2,1)} fusion(bf16[256,1600]{0,1:T(8,128)(2,1)S(1)} %copy-done.52, bf16[256,1600]{0,1:T(8,128)(2,1)S(1)} %copy-done.54, bf16[256,1600]{0,1:T(8,128)(2,1)S(1)} %copy-done.50, bf16[256,1600]{0,1:T(8,128)(2,1)S(1)} %bitcast.164, bf16[256,1600]{0,1:T(8,128)(2,1)S(1)} %get-tuple-element.257, ...), kind=kOutput, calls=%fused_computation.6 | convolution fusion | flops 5271654400 | bytes 11673600 | tf_op jit(solution)/shard_map/dot_general | solution.py:23
  269.1 6.3 %convolution_convert_fusion.1 = bf16[1600,1600]{1,0:T(8,128)(2,1)S(1)} fusion(bf16[1024,1600]{0,1:T(8,128)(2,1)S(1)} %copy-done.55, bf16[256,1600]{0,1:T(8,128)(2,1)S(1)} %get-tuple-element.197, bf16[256,1600]{0,1:T(8,128)(2,1)S(1)} %get-tuple-element.198, bf16[256,1600]{0,1:T(8,128)(2,1)S(1)} %get-tuple-element.199, ...), kind=kOutput, calls=%fused_computation.5 | convolution fusion | flops 5258547200 | bytes 11673600 | tf_op jit(solution)/shard_map/dot_general | solution.py:23
  279.2 7.8 %collective-permute-done.25 = bf16[256,1600]{0,1:T(8,128)(2,1)S(1)} collective-permute-done((bf16[256,1600]{0,1:T(8,128)(2,1)}, bf16[256,1600]{0,1:T(8,128)(2,1)S(1)}, u32[]{:S(2)}, u32[]{:S(2)}) %collective-permute-start.25) | collective-permute-done | bytes 819232 | tf_op jit(solution)/shard_map/ppermute | solution.py:433
  287.0 15.9 %collective-permute-done.26 = bf16[256,1600]{0,1:T(8,128)(2,1)S(1)} collective-permute-done((bf16[256,1600]{0,1:T(8,128)(2,1)S(1)}, bf16[256,1600]{0,1:T(8,128)(2,1)S(1)}, u32[]{:S(2)}, u32[]{:S(2)}) %collective-permute-start.26) | collective-permute-done | bytes 819232 | tf_op jit(solution)/shard_map/ppermute | solution.py:433
  334.0 29.2 %shard_map.277 = bf16[1024,1344]{1,0:T(8,128)(2,1)S(1)} custom-call(s32[4]{0:T(128)S(1)} %pad_add_fusion.1.info_ref, bf16[1024,1344]{1,0:T(8,128)(2,1)} %copy-done, bf16[1024,448]{1,0:T(8,128)(2,1)S(1)} %copy-done.1), custom_call_target="tpu_custom_call" | custom-call | flops 1 | bytes 1 | tf_op jit(solution)/shard_map/pallas_call | solution.py:200
  366.7 6.9 %convolution_convert_fusion = bf16[1600,1152]{1,0:T(8,128)(2,1)S(1)} fusion(bf16[1024,1344]{1,0:T(8,128)(2,1)S(1)} %shard_map.277, bf16[1024,1600]{0,1:T(8,128)(2,1)} %copy-done.25, f32[1600]{0:T(1024)S(1)} %get-tuple-element.191, f32[1600]{0:T(1024)S(1)} %get-tuple-element.192, f32[1024]{0:T(1024)S(1)} %add_rsqrt_fusion, f32[1024]{0:T(1024)S(1)} %broadcast_multiply_fusion), kind=kOutput, calls=%fused_computation.4 | convolution fusion | flops 3786547200 | bytes 9347072 | tf_op jit(solution)/shard_map/dot_general | solution.py:23
  397.2 7.5 %collective-permute-done.43 = bf16[208,1600]{1,0:T(8,128)(2,1)S(1)} collective-permute-done((bf16[208,1600]{1,0:T(8,128)(2,1)S(1)}, bf16[208,1600]{1,0:T(8,128)(2,1)S(1)}, u32[]{:S(2)}, u32[]{:S(2)}) %collective-permute-start.43) | collective-permute-done | bytes 665632 | tf_op jit(solution)/shard_map/ppermute | solution.py:433
  404.7 14.4 %collective-permute-done.42 = bf16[208,1600]{1,0:T(8,128)(2,1)S(1)} collective-permute-done((bf16[208,1600]{1,0:T(8,128)(2,1)S(1)}, bf16[208,1600]{1,0:T(8,128)(2,1)S(1)}, u32[]{:S(2)}, u32[]{:S(2)}) %collective-permute-start.42) | collective-permute-done | bytes 665632 | tf_op jit(solution)/shard_map/ppermute | solution.py:433
  425.2 10.9 %collective-permute-done.38 = bf16[208,1152]{1,0:T(8,128)(2,1)S(1)} collective-permute-done((bf16[208,1152]{1,0:T(8,128)(2,1)S(1)}, bf16[208,1152]{1,0:T(8,128)(2,1)S(1)}, u32[]{:S(2)}, u32[]{:S(2)}) %collective-permute-start.38) | collective-permute-done | bytes 479264 | tf_op jit(solution)/shard_map/ppermute | solution.py:433
  436.1 9.4 %collective-permute-done.37 = bf16[208,1152]{1,0:T(8,128)(2,1)S(1)} collective-permute-done((bf16[208,1152]{1,0:T(8,128)(2,1)S(1)}, bf16[208,1152]{1,0:T(8,128)(2,1)S(1)}, u32[]{:S(2)}, u32[]{:S(2)}) %collective-permute-start.37) | collective-permute-done | bytes 479264 | tf_op jit(solution)/shard_map/ppermute | solution.py:433
  455.3 6.1 convolution_convert_fusion.13
  488.7 13.0 %collective-permute-done.44 = bf16[256,1600]{0,1:T(8,128)(2,1)} collective-permute-done((bf16[256,1600]{0,1:T(8,128)(2,1)}, bf16[256,1600]{0,1:T(8,128)(2,1)}, u32[]{:S(2)}, u32[]{:S(2)}) %collective-permute-start.44) | collective-permute-done | bytes 819232 | tf_op jit(solution)/shard_map/ppermute | solution.py:433
  503.0 33.2 %collective-permute-done.45 = bf16[256,1600]{0,1:T(8,128)(2,1)} collective-permute-done((bf16[256,1600]{0,1:T(8,128)(2,1)}, bf16[256,1600]{0,1:T(8,128)(2,1)}, u32[]{:S(2)}, u32[]{:S(2)}) %collective-permute-start.45) | collective-permute-done | bytes 819232 | tf_op jit(solution)/shard_map/ppermute | solution.py:433
  536.2 6.7 %fusion.18 = (f32[256]{0:T(256)S(1)}, f32[1600]{0:T(1024)S(1)}, f32[256]{0:T(256)S(1)}, f32[1600]{0:T(1024)S(1)}, f32[256,1600]{0,1:T(8,128)}) fusion(f32[1600]{0:T(1024)S(1)} %get-tuple-element.192, f32[256]{0:T(256)S(1)} %copy-done.70, f32[256]{0:T(256)S(1)} %copy-done.61, bf16[1,256,1600]{1,2,0:T(8,128)(2,1)} %param.16, ...), kind=kOutput, calls=%fused_computation.69 | convolution fusion | flops 1107554816 | bytes 10164992 | tf_op jit(solution)/shard_map/dot_general | solution.py:23
  571.1 26.4 %all-reduce.6.cloned.1.call-done.refs_0_ = bf16[208,6400]{1,0:T(8,128)(2,1)} async-done(((bf16[208,6400]{1,0:T(8,128)(2,1)}), bf16[208,6400]{1,0:T(8,128)(2,1)}) %all-reduce.6.cloned.1.call-update) | async-done | bytes 2662416 | tf_op jit(solution)/shard_map/psum | solution.py:692
  (441 shorter events, 280.1 us)
Async XLA Ops:
  7.2 149.7 %all-gather.2.cloned.1.call-start = ((), (), s32[]{:S(2)}) async-start(), calls=%async_computation | async-start | bytes 4096000 | tf_op jit(solution)/shard_map/all_gather | solution.py:557
  7.2 49.8 %collective-permute-start.4 = (bf16[256,1600]{0,1:T(8,128)(2,1)}, bf16[256,1600]{0,1:T(8,128)(2,1)}, u32[]{:S(2)}, u32[]{:S(2)}) collective-permute-start(bf16[256,1600]{0,1:T(8,128)(2,1)} %bitcast.150), channel_id=1, source_target_pairs={{0,16},{8,24},{16,0},{24,8},{1,17},{9,25},{17,1},{25,9},{2,18},{10... | collective-permute-start | bytes 2457608 | tf_op jit(solution)/shard_map/ppermute | solution.py:433
  10.3 46.8 %collective-permute-start.3 = (bf16[256,1600]{0,1:T(8,128)(2,1)}, bf16[256,1600]{0,1:T(8,128)(2,1)}, u32[]{:S(2)}, u32[]{:S(2)}) collective-permute-start(bf16[256,1600]{0,1:T(8,128)(2,1)} %bitcast.151), channel_id=1, source_target_pairs={{0,8},{8,0},{16,24},{24,16},{1,9},{9,1},{17,25},{25,17},{2,10},{10... | collective-permute-start | bytes 2457608 | tf_op jit(solution)/shard_map/ppermute | solution.py:433
  22.9 34.1 %collective-permute-start.2 = (bf16[224,1344]{1,0:T(8,128)(2,1)}, bf16[224,1344]{1,0:T(8,128)(2,1)S(1)}, u32[]{:S(2)}, u32[]{:S(2)}) collective-permute-start(bf16[224,1344]{1,0:T(8,128)(2,1)} %get-tuple-element.99), channel_id=1, source_target_pairs={{0,24},{8,16},{16,8},{24,0},{1,25},{9,17},{17,9},{25,1},{2,26},{10... | collective-permute-start | bytes 1806344 | tf_op jit(solution)/shard_map/ppermute | solution.py:433
  58.8 51.1 %collective-permute-start.9 = (bf16[208,1600]{1,0:T(8,128)(2,1)}, bf16[208,1600]{1,0:T(8,128)(2,1)}, u32[]{:S(2)}, u32[]{:S(2)}) collective-permute-start(bf16[208,1600]{1,0:T(8,128)(2,1)} %constant_dynamic-slice_fusion.11), channel_id=1, source_target_pairs={{0,16},{8,24},{16,0},{24,8},{1,17},{9,25},{17,1},{25,9},{2,18},{10... | collective-permute-start | bytes 1996808 | tf_op jit(solution)/shard_map/ppermute | solution.py:433
  60.4 49.5 %collective-permute-start.8 = (bf16[208,1600]{1,0:T(8,128)(2,1)}, bf16[208,1600]{1,0:T(8,128)(2,1)}, u32[]{:S(2)}, u32[]{:S(2)}) collective-permute-start(bf16[208,1600]{1,0:T(8,128)(2,1)} %constant_dynamic-slice_fusion.11), channel_id=1, source_target_pairs={{0,8},{8,0},{16,24},{24,16},{1,9},{9,1},{17,25},{25,17},{2,10},{10... | collective-permute-start | bytes 1996808 | tf_op jit(solution)/shard_map/ppermute | solution.py:433
  64.9 314.4 %all-reduce.8.cloned.1.call-start = ((), (), s32[]{:S(2)}) async-start(), calls=%async_computation.3 | async-start | bytes 10649600 | tf_op jit(solution)/shard_map/psum | solution.py:644
  148.8 36.1 %collective-permute-start.21 = (bf16[336,1600]{1,0:T(8,128)(2,1)S(1)}, bf16[336,1600]{1,0:T(8,128)(2,1)S(1)}, u32[]{:S(2)}, u32[]{:S(2)}) collective-permute-start(bf16[336,1600]{1,0:T(8,128)(2,1)S(1)} %constant_dynamic-update-slice_fusion.5.mine), channel_id=1, source_target_pairs={{0,2},{2,0},{4,6},{6,4},{1,3},{3,1},{5,7},{7,5},{8,10},{10,8},{12,... | collective-permute-start | bytes 3225608 | tf_op jit(solution)/shard_map/ppermute | solution.py:436
  252.4 236.2 %all-reduce.4.cloned.1.call-start = ((), (), s32[]{:S(2)}) async-start(), calls=%async_computation.1 | async-start | bytes 5537792 | tf_op jit(solution)/shard_map/psum | solution.py:671
  266.7 36.2 %collective-permute-start.26 = (bf16[256,1600]{0,1:T(8,128)(2,1)S(1)}, bf16[256,1600]{0,1:T(8,128)(2,1)S(1)}, u32[]{:S(2)}, u32[]{:S(2)}) collective-permute-start(bf16[256,1600]{0,1:T(8,128)(2,1)S(1)} %convolution_convert_fusion.9), channel_id=1, source_target_pairs={{0,16},{8,24},{16,0},{24,8},{1,17},{9,25},{17,1},{25,9},{2,18},{10... | collective-permute-start | bytes 2457608 | tf_op jit(solution)/shard_map/ppermute | solution.py:433
  268.1 34.8 %collective-permute-start.27 = (bf16[256,1600]{0,1:T(8,128)(2,1)S(1)}, bf16[256,1600]{0,1:T(8,128)(2,1)S(1)}, u32[]{:S(2)}, u32[]{:S(2)}) collective-permute-start(bf16[256,1600]{0,1:T(8,128)(2,1)S(1)} %convolution_convert_fusion.8), channel_id=1, source_target_pairs={{0,24},{8,16},{16,8},{24,0},{1,25},{9,17},{17,9},{25,1},{2,26},{10... | collective-permute-start | bytes 2457608 | tf_op jit(solution)/shard_map/ppermute | solution.py:433
  275.7 39.4 %collective-permute-start.31 = (bf16[4,208,1600]{2,1,0:T(8,128)(2,1)S(1)}, bf16[4,208,1600]{2,1,0:T(8,128)(2,1)S(1)}, u32[]{:S(2)}, u32[]{:S(2)}) collective-permute-start(bf16[4,208,1600]{2,1,0:T(8,128)(2,1)S(1)} %constant_dynamic-slice_fusion.7), channel_id=1, source_target_pairs={{0,1},{1,0},{2,3},{3,2},{4,5},{5,4},{6,7},{7,6},{8,9},{9,8},{10,11... | collective-permute-start | bytes 7987208 | tf_op jit(solution)/shard_map/ppermute | solution.py:439
  324.1 39.1 %collective-permute-start.34 = (bf16[208,1600]{1,0:T(8,128)(2,1)}, bf16[208,1600]{1,0:T(8,128)(2,1)}, u32[]{:S(2)}, u32[]{:S(2)}) collective-permute-start(bf16[208,1600]{1,0:T(8,128)(2,1)} %get-tuple-element.208), channel_id=1, source_target_pairs={{0,24},{8,16},{16,8},{24,0},{1,25},{9,17},{17,9},{25,1},{2,26},{10... | collective-permute-start | bytes 1996808 | tf_op jit(solution)/shard_map/ppermute | solution.py:433
  325.6 37.7 %collective-permute-start.33 = (bf16[208,1600]{1,0:T(8,128)(2,1)}, bf16[208,1600]{1,0:T(8,128)(2,1)}, u32[]{:S(2)}, u32[]{:S(2)}) collective-permute-start(bf16[208,1600]{1,0:T(8,128)(2,1)} %get-tuple-element.209), channel_id=1, source_target_pairs={{0,16},{8,24},{16,0},{24,8},{1,17},{9,25},{17,1},{25,9},{2,18},{10... | collective-permute-start | bytes 1996808 | tf_op jit(solution)/shard_map/ppermute | solution.py:433
  326.2 37.1 %collective-permute-start.32 = (bf16[208,1600]{1,0:T(8,128)(2,1)}, bf16[208,1600]{1,0:T(8,128)(2,1)}, u32[]{:S(2)}, u32[]{:S(2)}) collective-permute-start(bf16[208,1600]{1,0:T(8,128)(2,1)} %get-tuple-element.210), channel_id=1, source_target_pairs={{0,8},{8,0},{16,24},{24,16},{1,9},{9,1},{17,25},{25,17},{2,10},{10... | collective-permute-start | bytes 1996808 | tf_op jit(solution)/shard_map/ppermute | solution.py:433
  329.4 52.2 %collective-permute-start.40 = (bf16[4,208,1600]{2,1,0:T(8,128)(2,1)}, bf16[4,208,1600]{2,1,0:T(8,128)(2,1)}, u32[]{:S(2)}, u32[]{:S(2)}) collective-permute-start(bf16[4,208,1600]{2,1,0:T(8,128)(2,1)} %constant_dynamic-slice_fusion.4), channel_id=1, source_target_pairs={{0,1},{1,0},{2,3},{3,2},{4,5},{5,4},{6,7},{7,6},{8,9},{9,8},{10,11... | collective-permute-start | bytes 7987208 | tf_op jit(solution)/shard_map/ppermute | solution.py:439
  376.9 42.2 %collective-permute-start.35 = (bf16[4,208,1152]{2,1,0:T(8,128)(2,1)}, bf16[4,208,1152]{2,1,0:T(8,128)(2,1)}, u32[]{:S(2)}, u32[]{:S(2)}) collective-permute-start(bf16[4,208,1152]{2,1,0:T(8,128)(2,1)} %constant_dynamic-slice_fusion.6), channel_id=1, source_target_pairs={{0,1},{1,0},{2,3},{3,2},{4,5},{5,4},{6,7},{7,6},{8,9},{9,8},{10,11... | collective-permute-start | bytes 5750792 | tf_op jit(solution)/shard_map/ppermute | solution.py:439
  379.4 218.2 %all-reduce.6.cloned.1.call-start = ((), (), s32[]{:S(2)}) async-start(), calls=%async_computation.2 | async-start | bytes 5324800 | tf_op jit(solution)/shard_map/psum | solution.py:692
  386.7 32.4 %collective-permute-start.42 = (bf16[208,1600]{1,0:T(8,128)(2,1)S(1)}, bf16[208,1600]{1,0:T(8,128)(2,1)S(1)}, u32[]{:S(2)}, u32[]{:S(2)}) collective-permute-start(bf16[208,1600]{1,0:T(8,128)(2,1)S(1)} %get-tuple-element.205), channel_id=1, source_target_pairs={{0,16},{8,24},{16,0},{24,8},{1,17},{9,25},{17,1},{25,9},{2,18},{10... | collective-permute-start | bytes 1996808 | tf_op jit(solution)/shard_map/ppermute | solution.py:433
  462.7 80.4 %collective-permute-start.53 = (bf16[256,1600]{0,1:T(8,128)(2,1)}, bf16[256,1600]{0,1:T(8,128)(2,1)}, u32[]{:S(2)}, u32[]{:S(2)}) collective-permute-start(bf16[256,1600]{0,1:T(8,128)(2,1)} %convolution_convert_fusion.13), channel_id=1, source_target_pairs={{0,8},{8,0},{16,24},{24,16},{1,9},{9,1},{17,25},{25,17},{2,10},{10... | collective-permute-start | bytes 2457608 | tf_op jit(solution)/shard_map/ppermute | solution.py:433
  463.2 79.9 %collective-permute-start.54 = (bf16[256,1600]{0,1:T(8,128)(2,1)}, bf16[256,1600]{0,1:T(8,128)(2,1)}, u32[]{:S(2)}, u32[]{:S(2)}) collective-permute-start(bf16[256,1600]{0,1:T(8,128)(2,1)} %convolution_convert_fusion.12), channel_id=1, source_target_pairs={{0,16},{8,24},{16,0},{24,8},{1,17},{9,25},{17,1},{25,9},{2,18},{10... | collective-permute-start | bytes 2457608 | tf_op jit(solution)/shard_map/ppermute | solution.py:433
  475.1 61.0 %collective-permute-start.45 = (bf16[256,1600]{0,1:T(8,128)(2,1)}, bf16[256,1600]{0,1:T(8,128)(2,1)}, u32[]{:S(2)}, u32[]{:S(2)}) collective-permute-start(bf16[256,1600]{0,1:T(8,128)(2,1)} %convolution_convert_fusion.6), channel_id=1, source_target_pairs={{0,16},{8,24},{16,0},{24,8},{1,17},{9,25},{17,1},{25,9},{2,18},{10... | collective-permute-start | bytes 2457608 | tf_op jit(solution)/shard_map/ppermute | solution.py:433
  479.1 57.1 %collective-permute-start.46 = (bf16[256,1600]{0,1:T(8,128)(2,1)}, bf16[256,1600]{0,1:T(8,128)(2,1)}, u32[]{:S(2)}, u32[]{:S(2)}) collective-permute-start(bf16[256,1600]{0,1:T(8,128)(2,1)} %convolution_convert_fusion.5), channel_id=1, source_target_pairs={{0,24},{8,16},{16,8},{24,0},{1,25},{9,17},{17,9},{25,1},{2,26},{10... | collective-permute-start | bytes 2457608 | tf_op jit(solution)/shard_map/ppermute | solution.py:433
  501.7 41.4 %collective-permute-start.55 = (bf16[256,1600]{0,1:T(8,128)(2,1)}, bf16[256,1600]{0,1:T(8,128)(2,1)}, u32[]{:S(2)}, u32[]{:S(2)}) collective-permute-start(bf16[256,1600]{0,1:T(8,128)(2,1)} %convolution_convert_fusion.11), channel_id=1, source_target_pairs={{0,24},{8,16},{16,8},{24,0},{1,25},{9,17},{17,9},{25,1},{2,26},{10... | collective-permute-start | bytes 2457608 | tf_op jit(solution)/shard_map/ppermute | solution.py:433
  (123 other events, 2352.0 us)
Sparse Core Ops, SparseCore 0:
  65.0 57.6 all-gather.1
  252.5 119.3 all-reduce.7
  379.5 109.1 all-reduce.3
  491.5 106.0 all-reduce.5

commit v2 on v0

--- a/solution.py
+++ b/solution.py
@@ -580,7 +580,8 @@
     fc_got = [swap(fc_sent[d], d) for d in range(1, n)]
     info = jnp.concatenate([lengths[0], me.astype(jnp.int32)[None]])
     mixed_heads = attention_fwd(info, qkv, n, heads)
-    mixed_heads, proj_parts, fc_got = after((mixed_heads, proj_parts, fc_got))
+    mixed_heads, proj_parts, fc_first = after((mixed_heads, proj_parts, fc_got[:-1]))
+    fc_got = list(fc_first) + fc_got[-1:]
     if by_parts:
         fc_mine = jnp.concatenate(fc_got)
         fc_near = swap_plane(fc_mine)
@@ -658,6 +659,7 @@
         [pick(fc_halves, me)] + [swap(pick(fc_halves, me ^ d), d) for d in range(1, n)]
     )
     fc_sum = lax.psum(fc_parts, "plane")
+    sum_out_weight = after(sum_out_weight, fc_parts).astype(F32)
     grad_fc_bias = jnp.sum(d_hidden.astype(F32), axis=0)
 
     d_qkv = attention_bwd(info, qkv, jnp.concatenate(dmix_parts, axis=0), n, heads)
@@ -740,16 +742,25 @@
         lane = 3 * main + part * spare
         return jnp.concatenate([whole[: n * main], d_once_sum[lane : lane + spare]])
 
+    early = after(
+        (
+            jnp.sum(d_branch.astype(F32), axis=0),
+            jnp.sum(e * xhat_two, axis=0),
+            jnp.sum(e, axis=0),
+            jnp.sum(own_cot.astype(F32), axis=0),
+        ),
+        attn_parts,
+    )
     small_grads = jnp.stack(
         [
             vector_of(0),
             vector_of(2),
-            jnp.sum(d_branch.astype(F32), axis=0),
+            early[0],
             jnp.sum(f * xhat_own, axis=0),
             jnp.sum(f, axis=0),
-            jnp.sum(e * xhat_two, axis=0),
-            jnp.sum(e, axis=0),
-            jnp.sum(own_cot.astype(F32), axis=0),
+            early[1],
+            early[2],
+            early[3],
         ]
     )
     small_grads = small_grads.reshape(8, n, own_rows).transpose(1, 0, 2)
@@ -764,7 +775,6 @@
             small_own, "plane", [(i, i ^ hop) for i in range(planes)]
         )
         hop *= 2
-    sum_out_weight = sum_out_weight.astype(F32)
     attn_sum, small_own, output, input_grad, sum_fc_weight, sum_out_weight = after(
         (attn_sum, small_own, output, input_grad, sum_fc_weight, sum_out_weight)
     )

time: 628 us -> 614 us (0.978)
  matrix products: 128 us -> 120 us
    dot_general x15, matrix products: 77.8 us -> 69.2 us  [dot(): lax.dot_general(left, right, (dims, ((), ())), preferred_element_type=F32)]
    unnamed x205 -> x201, local copies, waits for them, and re-layouts: 25.9 us -> 26.8 us
  transfers between devices with their start and end apart: 62 -> 62, of which waited for: 24 -> 28; matrix products, arithmetic and copies ran while one was open for 31% -> 29% of each run, Pallas kernels for 10% -> 11%
where the time goes in v2:
time: 614 us; the launch traced here: 605 us
  waiting for transfers between devices  234 us (38%)
  matrix products  120 us (20%)
  Pallas kernels  74.5 us (12%)
  starting transfers between devices  59 us (10%)
  local copies, waits for them, and re-layouts  51 us (8%)
  other arithmetic  49.7 us (8%)
  between operations  15.6 us (3%)
    ppermute x45, waiting for transfers between devices, swap(): return lax.ppermute(value, 'shard', [(i, i ^ d) for i in range(n)])  187 us
    dot_general x15, matrix products, dot(): lax.dot_general(left, right, (dims, ((), ())), preferred_element_type=F32)  69.2 us
    ppermute x45, starting transfers between devices, swap(): return lax.ppermute(value, 'shard', [(i, i ^ d) for i in range(n)])  52.8 us
    pallas_call x2, Pallas kernels, vmem_call(): pl.pallas_call(kernel, out_shape=out_shape, in_specs=[pl.BlockSpec(memory...  43.4 us
    pallas_call x7, Pallas kernels, local_call(): pl.pallas_call(kernel, out_shape=out_shape, in_specs=[pl.BlockSpec(memory...  31.1 us
    unnamed x201, local copies, waits for them, and re-layouts  26.8 us
    psum x1, waiting for transfers between devices, body(): attn_sum = lax.psum(after(attn_parts, fc_sum), 'plane')  26.3 us
    dot_general x4, matrix products, body(): jnp.dot(block(late_active, d), out_weight, preferred_element_type=F32)  18.8 us
  transfers between devices with their start and end apart: 62, of which 28 were waited for; matrix products, arithmetic and copies ran while one was open for 29% of the time, Pallas kernels for 11%

profile of v2, /device:TPU:0, one launch (start us, length us, event | category | flops | bytes accessed | tf_op | source)
XLA Modules:
  0.0 604.5 jit_solution(2565208814301093457)
XLA Ops:
  27.8 17.4 %collective-permute-done.refs_1_ = bf16[224,1344]{1,0:T(8,128)(2,1)S(1)} collective-permute-done((bf16[224,1344]{1,0:T(8,128)(2,1)}, bf16[224,1344]{1,0:T(8,128)(2,1)S(1)}, u32[]{:S(2)}, u32[]{:S(2)}) %collective-permute-start) | collective-permute-done | bytes 602144 | tf_op jit(solution)/shard_map/ppermute | solution.py:433
  45.2 11.8 %collective-permute-done.2.refs_3_ = bf16[224,1344]{1,0:T(8,128)(2,1)S(1)} collective-permute-done((bf16[224,1344]{1,0:T(8,128)(2,1)}, bf16[224,1344]{1,0:T(8,128)(2,1)S(1)}, u32[]{:S(2)}, u32[]{:S(2)}) %collective-permute-start.2) | collective-permute-done | bytes 602144 | tf_op jit(solution)/shard_map/ppermute | solution.py:433
  74.4 18.6 %collective-permute-done.5 = bf16[128,1600]{0,1:T(8,128)(2,1)S(1)} collective-permute-done((bf16[128,1600]{0,1:T(8,128)(2,1)}, bf16[128,1600]{0,1:T(8,128)(2,1)S(1)}, u32[]{:S(2)}, u32[]{:S(2)}) %collective-permute-start.5) | collective-permute-done | bytes 409632 | tf_op jit(solution)/shard_map/ppermute | solution.py:433
  100.8 9.3 %add_convert_fusion.qkv_ref = bf16[1024,1344]{1,0:T(8,128)(2,1)S(1)} fusion(bf16[1600,1344]{1,0:T(8,128)(2,1)} %get-tuple-element.98, f32[1344]{0:T(1024)S(1)} %concatenate.72, bf16[1024,1600]{0,1:T(8,128)(2,1)} %copy-done.25, f32[1600]{0:T(1024)S(1)} %get-tuple-element.173, f32[1600]{0:T(1024)S(1)} %get-tuple-element.174, f32[1024]{0:T(1024)S(1)} %add_rsqrt_fusion, ...), kind=kOutput, calls=%fused_computation.14 | convolution fusion | flops 4416602112 | bytes 10356480 | tf_op jit(solution)/shard_map/dot_general | solution.py:577
  116.7 14.2 %shard_map.274 = bf16[1024,448]{1,0:T(8,128)(2,1)S(1)} custom-call(s32[4]{0:T(128)S(1)} %pad_add_fusion.1.info_ref, bf16[1024,1344]{1,0:T(8,128)(2,1)S(1)} %add_convert_fusion.qkv_ref), custom_call_target="tpu_custom_call" | custom-call | flops 1 | bytes 1 | tf_op jit(solution)/shard_map/pallas_call | solution.py:200
  145.2 7.3 %collective-permute-done.20 = bf16[112,1600]{1,0:T(8,128)(2,1)S(1)} collective-permute-done((bf16[112,1600]{1,0:T(8,128)(2,1)S(1)}, bf16[112,1600]{1,0:T(8,128)(2,1)S(1)}, u32[]{:S(2)}, u32[]{:S(2)}) %collective-permute-start.20) | collective-permute-done | bytes 358432 | tf_op jit(solution)/shard_map/ppermute | solution.py:433
  172.0 6.4 %collective-permute-done.21.near = bf16[336,1600]{1,0:T(8,128)(2,1)S(1)} collective-permute-done((bf16[336,1600]{1,0:T(8,128)(2,1)S(1)}, bf16[336,1600]{1,0:T(8,128)(2,1)S(1)}, u32[]{:S(2)}, u32[]{:S(2)}) %collective-permute-start.21) | collective-permute-done | bytes 1075232 | tf_op jit(solution)/shard_map/ppermute | solution.py:436
  179.7 10.6 %convolution_convert_fusion.4 = bf16[1024,1600]{0,1:T(8,128)(2,1)} fusion(bf16[1600,1600]{1,0:T(8,128)(2,1)} %param.30, bf16[256,1600]{0,1:T(8,128)(2,1)S(1)} %get-tuple-element.184, bf16[256,1600]{0,1:T(8,128)(2,1)S(1)} %get-tuple-element.185, bf16[256,1600]{0,1:T(8,128)(2,1)S(1)} %get-tuple-element.183, bf16[256,1600]{0,1:T(8,128)(2,1)S(1)} %bitcast.163), kind=kOutput, calls=%fused_computation.19 | convolution fusion | flops 5257625600 | bytes 11673600 | tf_op jit(solution)/shard_map/dot_general | solution.py:23
  194.5 8.0 %collective-permute-done.23 = bf16[128,1600]{0,1:T(8,128)(2,1)S(1)} collective-permute-done((bf16[128,1600]{0,1:T(8,128)(2,1)S(1)}, bf16[128,1600]{0,1:T(8,128)(2,1)S(1)}, u32[]{:S(2)}, u32[]{:S(2)}) %collective-permute-start.23) | collective-permute-done | bytes 409632 | tf_op jit(solution)/shard_map/ppermute | solution.py:433
  207.5 6.4 %multiply_convert_fusion.5 = (bf16[256,1600]{0,1:T(8,128)(2,1)S(1)}, f32[256,1600]{0,1:T(8,128)}) fusion(f32[1600]{0:T(1024)S(1)} %copy-done.70, bf16[256,1600]{0,1:T(8,128)(2,1)S(1)} %collective-permute-done.19, bf16[1600,1600]{1,0:T(8,128)(2,1)} %shard_map.276), kind=kOutput, calls=%fused_computation.112 | convolution fusion | flops 1314816000 | bytes 8403200 | tf_op jit(solution)/shard_map/dot_general | solution.py:622
  226.2 9.0 %convolution_convert_fusion.2 = bf16[1600,1600]{1,0:T(8,128)(2,1)} fusion(bf16[256,1600]{0,1:T(8,128)(2,1)S(1)} %copy-done.55, bf16[256,1600]{0,1:T(8,128)(2,1)S(1)} %copy-done.57, bf16[256,1600]{0,1:T(8,128)(2,1)S(1)} %copy-done.53, bf16[256,1600]{0,1:T(8,128)(2,1)S(1)} %bitcast.164, bf16[256,1600]{0,1:T(8,128)(2,1)S(1)} %get-tuple-element.233, ...), kind=kOutput, calls=%fused_computation.6 | convolution fusion | flops 5271654400 | bytes 11673600 | tf_op jit(solution)/shard_map/dot_general | solution.py:23
  237.1 6.2 %multiply_convert_fusion = (bf16[256,1600]{0,1:T(8,128)(2,1)S(1)}, bf16[256,1600]{0,1:T(8,128)(2,1)S(1)}, bf16[256,1600]{0,1:T(8,128)(2,1)S(1)}, bf16[256,1600]{0,1:T(8,128)(2,1)S(1)}) fusion(f32[256,1600]{0,1:T(8,128)} %get-tuple-element.234, bf16[1024,1600]{0,1:T(8,128)(2,1)S(1)} %copy-done.38, f32[256,1600]{0,1:T(8,128)} %get-tuple-element.236, ...), kind=kLoop, calls=%fused_computation.107 | loop fusion | flops 36044800 | bytes 13107200 | tf_op jit(solution)/shard_map/convert_element_type | solution.py:637
  254.6 7.8 %convolution_convert_fusion.1 = bf16[1600,1600]{1,0:T(8,128)(2,1)S(1)} fusion(bf16[1024,1600]{0,1:T(8,128)(2,1)} %constant_dynamic-update-slice_fusion.8, bf16[256,1600]{0,1:T(8,128)(2,1)S(1)} %get-tuple-element.179, bf16[256,1600]{0,1:T(8,128)(2,1)S(1)} %get-tuple-element.180, bf16[256,1600]{0,1:T(8,128)(2,1)S(1)} %get-tuple-element.181, ...), kind=kOutput, calls=%fused_computation.5 | convolution fusion | flops 5258547200 | bytes 11673600 | tf_op jit(solution)/shard_map/dot_general | solution.py:23
  272.2 16.3 %collective-permute-done.26 = bf16[256,1600]{0,1:T(8,128)(2,1)S(1)} collective-permute-done((bf16[256,1600]{0,1:T(8,128)(2,1)S(1)}, bf16[256,1600]{0,1:T(8,128)(2,1)S(1)}, u32[]{:S(2)}, u32[]{:S(2)}) %collective-permute-start.26) | collective-permute-done | bytes 819232 | tf_op jit(solution)/shard_map/ppermute | solution.py:433
  321.2 29.3 %shard_map.277 = bf16[1024,1344]{1,0:T(8,128)(2,1)S(1)} custom-call(s32[4]{0:T(128)S(1)} %pad_add_fusion.1.info_ref, bf16[1024,1344]{1,0:T(8,128)(2,1)} %copy-done, bf16[1024,448]{1,0:T(8,128)(2,1)S(1)} %copy-done.1), custom_call_target="tpu_custom_call" | custom-call | flops 1 | bytes 1 | tf_op jit(solution)/shard_map/pallas_call | solution.py:200
  353.9 6.9 %convolution_convert_fusion = bf16[1600,1152]{1,0:T(8,128)(2,1)S(1)} fusion(bf16[1024,1344]{1,0:T(8,128)(2,1)S(1)} %shard_map.277, bf16[1024,1600]{0,1:T(8,128)(2,1)} %copy-done.25, f32[1600]{0:T(1024)S(1)} %copy-done.67, f32[1600]{0:T(1024)S(1)} %get-tuple-element.174, f32[1024]{0:T(1024)S(1)} %copy-done.75, f32[1024]{0:T(1024)S(1)} %broadcast_multiply_fusion), kind=kOutput, calls=%fused_computation.4 | convolution fusion | flops 3786547200 | bytes 9347072 | tf_op jit(solution)/shard_map/dot_general | solution.py:23
  384.9 7.5 %collective-permute-done.43 = bf16[208,1600]{1,0:T(8,128)(2,1)S(1)} collective-permute-done((bf16[208,1600]{1,0:T(8,128)(2,1)S(1)}, bf16[208,1600]{1,0:T(8,128)(2,1)S(1)}, u32[]{:S(2)}, u32[]{:S(2)}) %collective-permute-start.43) | collective-permute-done | bytes 665632 | tf_op jit(solution)/shard_map/ppermute | solution.py:433
  392.4 13.8 %collective-permute-done.42 = bf16[208,1600]{1,0:T(8,128)(2,1)S(1)} collective-permute-done((bf16[208,1600]{1,0:T(8,128)(2,1)S(1)}, bf16[208,1600]{1,0:T(8,128)(2,1)S(1)}, u32[]{:S(2)}, u32[]{:S(2)}) %collective-permute-start.42) | collective-permute-done | bytes 665632 | tf_op jit(solution)/shard_map/ppermute | solution.py:433
  412.4 10.9 %collective-permute-done.38 = bf16[208,1152]{1,0:T(8,128)(2,1)S(1)} collective-permute-done((bf16[208,1152]{1,0:T(8,128)(2,1)S(1)}, bf16[208,1152]{1,0:T(8,128)(2,1)S(1)}, u32[]{:S(2)}, u32[]{:S(2)}) %collective-permute-start.38) | collective-permute-done | bytes 479264 | tf_op jit(solution)/shard_map/ppermute | solution.py:433
  423.3 9.4 %collective-permute-done.37 = bf16[208,1152]{1,0:T(8,128)(2,1)S(1)} collective-permute-done((bf16[208,1152]{1,0:T(8,128)(2,1)S(1)}, bf16[208,1152]{1,0:T(8,128)(2,1)S(1)}, u32[]{:S(2)}, u32[]{:S(2)}) %collective-permute-start.37) | collective-permute-done | bytes 479264 | tf_op jit(solution)/shard_map/ppermute | solution.py:433
  475.8 13.1 %collective-permute-done.44 = bf16[256,1600]{0,1:T(8,128)(2,1)} collective-permute-done((bf16[256,1600]{0,1:T(8,128)(2,1)}, bf16[256,1600]{0,1:T(8,128)(2,1)}, u32[]{:S(2)}, u32[]{:S(2)}) %collective-permute-start.44) | collective-permute-done | bytes 819232 | tf_op jit(solution)/shard_map/ppermute | solution.py:433
  490.4 33.0 %collective-permute-done.45 = bf16[256,1600]{0,1:T(8,128)(2,1)} collective-permute-done((bf16[256,1600]{0,1:T(8,128)(2,1)}, bf16[256,1600]{0,1:T(8,128)(2,1)}, u32[]{:S(2)}, u32[]{:S(2)}) %collective-permute-start.45) | collective-permute-done | bytes 819232 | tf_op jit(solution)/shard_map/ppermute | solution.py:433
  523.4 6.7 %fusion.18 = (f32[256]{0:T(256)S(1)}, f32[1600]{0:T(1024)S(1)}, f32[256]{0:T(256)S(1)}, f32[1600]{0:T(1024)S(1)}, f32[256,1600]{0,1:T(8,128)}) fusion(f32[1600]{0:T(1024)S(1)} %get-tuple-element.174, f32[256]{0:T(256)S(1)} %copy-done.76, f32[256]{0:T(256)S(1)} %copy-done.65, bf16[1,256,1600]{1,2,0:T(8,128)(2,1)} %param.16, ...), kind=kOutput, calls=%fused_computation.69 | convolution fusion | flops 1107554816 | bytes 10164992 | tf_op jit(solution)/shard_map/dot_general | solution.py:23
  558.4 26.3 %all-reduce.6.cloned.1.call-done.refs_0_ = bf16[208,6400]{1,0:T(8,128)(2,1)} async-done(((bf16[208,6400]{1,0:T(8,128)(2,1)}), bf16[208,6400]{1,0:T(8,128)(2,1)}) %all-reduce.6.cloned.1.call-update) | async-done | bytes 2662416 | tf_op jit(solution)/shard_map/psum | solution.py:682
  (448 shorter events, 282.8 us)
Async XLA Ops:
  7.2 153.4 %all-gather.2.cloned.1.call-start = ((), (), s32[]{:S(2)}) async-start(), calls=%async_computation | async-start | bytes 4096000 | tf_op jit(solution)/shard_map/all_gather | solution.py:557
  7.2 49.8 %collective-permute-start.4 = (bf16[256,1600]{0,1:T(8,128)(2,1)}, bf16[256,1600]{0,1:T(8,128)(2,1)}, u32[]{:S(2)}, u32[]{:S(2)}) collective-permute-start(bf16[256,1600]{0,1:T(8,128)(2,1)} %bitcast.150), channel_id=1, source_target_pairs={{0,16},{8,24},{16,0},{24,8},{1,17},{9,25},{17,1},{25,9},{2,18},{10... | collective-permute-start | bytes 2457608 | tf_op jit(solution)/shard_map/ppermute | solution.py:433
  10.3 46.8 %collective-permute-start.3 = (bf16[256,1600]{0,1:T(8,128)(2,1)}, bf16[256,1600]{0,1:T(8,128)(2,1)}, u32[]{:S(2)}, u32[]{:S(2)}) collective-permute-start(bf16[256,1600]{0,1:T(8,128)(2,1)} %bitcast.151), channel_id=1, source_target_pairs={{0,8},{8,0},{16,24},{24,16},{1,9},{9,1},{17,25},{25,17},{2,10},{10... | collective-permute-start | bytes 2457608 | tf_op jit(solution)/shard_map/ppermute | solution.py:433
  22.8 34.2 %collective-permute-start.2 = (bf16[224,1344]{1,0:T(8,128)(2,1)}, bf16[224,1344]{1,0:T(8,128)(2,1)S(1)}, u32[]{:S(2)}, u32[]{:S(2)}) collective-permute-start(bf16[224,1344]{1,0:T(8,128)(2,1)} %get-tuple-element.90), channel_id=1, source_target_pairs={{0,24},{8,16},{16,8},{24,0},{1,25},{9,17},{17,9},{25,1},{2,26},{10... | collective-permute-start | bytes 1806344 | tf_op jit(solution)/shard_map/ppermute | solution.py:433
  58.8 51.4 %collective-permute-start.9 = (bf16[208,1600]{1,0:T(8,128)(2,1)}, bf16[208,1600]{1,0:T(8,128)(2,1)}, u32[]{:S(2)}, u32[]{:S(2)}) collective-permute-start(bf16[208,1600]{1,0:T(8,128)(2,1)} %constant_dynamic-slice_fusion.11), channel_id=1, source_target_pairs={{0,16},{8,24},{16,0},{24,8},{1,17},{9,25},{17,1},{25,9},{2,18},{10... | collective-permute-start | bytes 1996808 | tf_op jit(solution)/shard_map/ppermute | solution.py:433
  60.4 49.7 %collective-permute-start.8 = (bf16[208,1600]{1,0:T(8,128)(2,1)}, bf16[208,1600]{1,0:T(8,128)(2,1)}, u32[]{:S(2)}, u32[]{:S(2)}) collective-permute-start(bf16[208,1600]{1,0:T(8,128)(2,1)} %constant_dynamic-slice_fusion.11), channel_id=1, source_target_pairs={{0,8},{8,0},{16,24},{24,16},{1,9},{9,1},{17,25},{25,17},{2,10},{10... | collective-permute-start | bytes 1996808 | tf_op jit(solution)/shard_map/ppermute | solution.py:433
  64.9 301.6 %all-reduce.8.cloned.1.call-start = ((), (), s32[]{:S(2)}) async-start(), calls=%async_computation.3 | async-start | bytes 10649600 | tf_op jit(solution)/shard_map/psum | solution.py:634
  235.2 240.6 %all-reduce.4.cloned.1.call-start = ((), (), s32[]{:S(2)}) async-start(), calls=%async_computation.1 | async-start | bytes 5537792 | tf_op jit(solution)/shard_map/psum | solution.py:661
  252.7 35.9 %collective-permute-start.26 = (bf16[256,1600]{0,1:T(8,128)(2,1)S(1)}, bf16[256,1600]{0,1:T(8,128)(2,1)S(1)}, u32[]{:S(2)}, u32[]{:S(2)}) collective-permute-start(bf16[256,1600]{0,1:T(8,128)(2,1)S(1)} %convolution_convert_fusion.9), channel_id=1, source_target_pairs={{0,16},{8,24},{16,0},{24,8},{1,17},{9,25},{17,1},{25,9},{2,18},{10... | collective-permute-start | bytes 2457608 | tf_op jit(solution)/shard_map/ppermute | solution.py:433
  254.2 35.1 %collective-permute-start.27 = (bf16[256,1600]{0,1:T(8,128)(2,1)S(1)}, bf16[256,1600]{0,1:T(8,128)(2,1)S(1)}, u32[]{:S(2)}, u32[]{:S(2)}) collective-permute-start(bf16[256,1600]{0,1:T(8,128)(2,1)S(1)} %convolution_convert_fusion.8), channel_id=1, source_target_pairs={{0,24},{8,16},{16,8},{24,0},{1,25},{9,17},{17,9},{25,1},{2,26},{10... | collective-permute-start | bytes 2457608 | tf_op jit(solution)/shard_map/ppermute | solution.py:433
  262.6 38.8 %collective-permute-start.31 = (bf16[4,208,1600]{2,1,0:T(8,128)(2,1)S(1)}, bf16[4,208,1600]{2,1,0:T(8,128)(2,1)S(1)}, u32[]{:S(2)}, u32[]{:S(2)}) collective-permute-start(bf16[4,208,1600]{2,1,0:T(8,128)(2,1)S(1)} %constant_dynamic-slice_fusion.7), channel_id=1, source_target_pairs={{0,1},{1,0},{2,3},{3,2},{4,5},{5,4},{6,7},{7,6},{8,9},{9,8},{10,11... | collective-permute-start | bytes 7987208 | tf_op jit(solution)/shard_map/ppermute | solution.py:439
  311.3 39.1 %collective-permute-start.34 = (bf16[208,1600]{1,0:T(8,128)(2,1)}, bf16[208,1600]{1,0:T(8,128)(2,1)}, u32[]{:S(2)}, u32[]{:S(2)}) collective-permute-start(bf16[208,1600]{1,0:T(8,128)(2,1)} %get-tuple-element.190), channel_id=1, source_target_pairs={{0,24},{8,16},{16,8},{24,0},{1,25},{9,17},{17,9},{25,1},{2,26},{10... | collective-permute-start | bytes 1996808 | tf_op jit(solution)/shard_map/ppermute | solution.py:433
  312.9 37.5 %collective-permute-start.33 = (bf16[208,1600]{1,0:T(8,128)(2,1)}, bf16[208,1600]{1,0:T(8,128)(2,1)}, u32[]{:S(2)}, u32[]{:S(2)}) collective-permute-start(bf16[208,1600]{1,0:T(8,128)(2,1)} %get-tuple-element.191), channel_id=1, source_target_pairs={{0,16},{8,24},{16,0},{24,8},{1,17},{9,25},{17,1},{25,9},{2,18},{10... | collective-permute-start | bytes 1996808 | tf_op jit(solution)/shard_map/ppermute | solution.py:433
  313.4 37.1 %collective-permute-start.32 = (bf16[208,1600]{1,0:T(8,128)(2,1)}, bf16[208,1600]{1,0:T(8,128)(2,1)}, u32[]{:S(2)}, u32[]{:S(2)}) collective-permute-start(bf16[208,1600]{1,0:T(8,128)(2,1)} %get-tuple-element.192), channel_id=1, source_target_pairs={{0,8},{8,0},{16,24},{24,16},{1,9},{9,1},{17,25},{25,17},{2,10},{10... | collective-permute-start | bytes 1996808 | tf_op jit(solution)/shard_map/ppermute | solution.py:433
  316.6 52.6 %collective-permute-start.40 = (bf16[4,208,1600]{2,1,0:T(8,128)(2,1)}, bf16[4,208,1600]{2,1,0:T(8,128)(2,1)}, u32[]{:S(2)}, u32[]{:S(2)}) collective-permute-start(bf16[4,208,1600]{2,1,0:T(8,128)(2,1)} %constant_dynamic-slice_fusion.4), channel_id=1, source_target_pairs={{0,1},{1,0},{2,3},{3,2},{4,5},{5,4},{6,7},{7,6},{8,9},{9,8},{10,11... | collective-permute-start | bytes 7987208 | tf_op jit(solution)/shard_map/ppermute | solution.py:439
  364.1 42.2 %collective-permute-start.35 = (bf16[4,208,1152]{2,1,0:T(8,128)(2,1)}, bf16[4,208,1152]{2,1,0:T(8,128)(2,1)}, u32[]{:S(2)}, u32[]{:S(2)}) collective-permute-start(bf16[4,208,1152]{2,1,0:T(8,128)(2,1)} %constant_dynamic-slice_fusion.6), channel_id=1, source_target_pairs={{0,1},{1,0},{2,3},{3,2},{4,5},{5,4},{6,7},{7,6},{8,9},{9,8},{10,11... | collective-permute-start | bytes 5750792 | tf_op jit(solution)/shard_map/ppermute | solution.py:439
  366.5 218.2 %all-reduce.6.cloned.1.call-start = ((), (), s32[]{:S(2)}) async-start(), calls=%async_computation.2 | async-start | bytes 5324800 | tf_op jit(solution)/shard_map/psum | solution.py:682
  374.6 31.7 %collective-permute-start.42 = (bf16[208,1600]{1,0:T(8,128)(2,1)S(1)}, bf16[208,1600]{1,0:T(8,128)(2,1)S(1)}, u32[]{:S(2)}, u32[]{:S(2)}) collective-permute-start(bf16[208,1600]{1,0:T(8,128)(2,1)S(1)} %get-tuple-element.187), channel_id=1, source_target_pairs={{0,16},{8,24},{16,0},{24,8},{1,17},{9,25},{17,1},{25,9},{2,18},{10... | collective-permute-start | bytes 1996808 | tf_op jit(solution)/shard_map/ppermute | solution.py:433
  449.9 80.4 %collective-permute-start.53 = (bf16[256,1600]{0,1:T(8,128)(2,1)}, bf16[256,1600]{0,1:T(8,128)(2,1)}, u32[]{:S(2)}, u32[]{:S(2)}) collective-permute-start(bf16[256,1600]{0,1:T(8,128)(2,1)} %convolution_convert_fusion.13), channel_id=1, source_target_pairs={{0,8},{8,0},{16,24},{24,16},{1,9},{9,1},{17,25},{25,17},{2,10},{10... | collective-permute-start | bytes 2457608 | tf_op jit(solution)/shard_map/ppermute | solution.py:433
  450.5 79.8 %collective-permute-start.54 = (bf16[256,1600]{0,1:T(8,128)(2,1)}, bf16[256,1600]{0,1:T(8,128)(2,1)}, u32[]{:S(2)}, u32[]{:S(2)}) collective-permute-start(bf16[256,1600]{0,1:T(8,128)(2,1)} %convolution_convert_fusion.12), channel_id=1, source_target_pairs={{0,16},{8,24},{16,0},{24,8},{1,17},{9,25},{17,1},{25,9},{2,18},{10... | collective-permute-start | bytes 2457608 | tf_op jit(solution)/shard_map/ppermute | solution.py:433
  456.9 32.0 %collective-permute-start.44 = (bf16[256,1600]{0,1:T(8,128)(2,1)}, bf16[256,1600]{0,1:T(8,128)(2,1)}, u32[]{:S(2)}, u32[]{:S(2)}) collective-permute-start(bf16[256,1600]{0,1:T(8,128)(2,1)} %convolution_convert_fusion.7), channel_id=1, source_target_pairs={{0,8},{8,0},{16,24},{24,16},{1,9},{9,1},{17,25},{25,17},{2,10},{10... | collective-permute-start | bytes 2457608 | tf_op jit(solution)/shard_map/ppermute | solution.py:433
  462.4 61.0 %collective-permute-start.45 = (bf16[256,1600]{0,1:T(8,128)(2,1)}, bf16[256,1600]{0,1:T(8,128)(2,1)}, u32[]{:S(2)}, u32[]{:S(2)}) collective-permute-start(bf16[256,1600]{0,1:T(8,128)(2,1)} %convolution_convert_fusion.6), channel_id=1, source_target_pairs={{0,16},{8,24},{16,0},{24,8},{1,17},{9,25},{17,1},{25,9},{2,18},{10... | collective-permute-start | bytes 2457608 | tf_op jit(solution)/shard_map/ppermute | solution.py:433
  466.3 57.1 %collective-permute-start.46 = (bf16[256,1600]{0,1:T(8,128)(2,1)}, bf16[256,1600]{0,1:T(8,128)(2,1)}, u32[]{:S(2)}, u32[]{:S(2)}) collective-permute-start(bf16[256,1600]{0,1:T(8,128)(2,1)} %convolution_convert_fusion.5), channel_id=1, source_target_pairs={{0,24},{8,16},{16,8},{24,0},{1,25},{9,17},{17,9},{25,1},{2,26},{10... | collective-permute-start | bytes 2457608 | tf_op jit(solution)/shard_map/ppermute | solution.py:433
  488.9 41.4 %collective-permute-start.55 = (bf16[256,1600]{0,1:T(8,128)(2,1)}, bf16[256,1600]{0,1:T(8,128)(2,1)}, u32[]{:S(2)}, u32[]{:S(2)}) collective-permute-start(bf16[256,1600]{0,1:T(8,128)(2,1)} %convolution_convert_fusion.11), channel_id=1, source_target_pairs={{0,24},{8,16},{16,8},{24,0},{1,25},{9,17},{17,9},{25,1},{2,26},{10... | collective-permute-start | bytes 2457608 | tf_op jit(solution)/shard_map/ppermute | solution.py:433
  (127 other events, 1738.9 us)
Sparse Core Ops, SparseCore 0:
  65.0 57.4 all-gather.1
  235.3 119.5 all-reduce.7
  366.6 109.0 all-reduce.3
  478.6 106.0 all-reduce.5

commit v3 on v2

--- a/solution.py
+++ b/solution.py
@@ -663,7 +663,7 @@
     grad_fc_bias = jnp.sum(d_hidden.astype(F32), axis=0)
 
     d_qkv = attention_bwd(info, qkv, jnp.concatenate(dmix_parts, axis=0), n, heads)
-    d_qkv, fc_parts = after((d_qkv, fc_parts))
+    d_qkv, fc_parts, sum_out_weight = after((d_qkv, fc_parts, sum_out_weight))
 
     grad_proj = rows_dot(mixed_low, d_branch).astype(BF).reshape(n, own_rows, D)
     proj_halves = after(core_halves(grad_proj), fc_parts)

time: 614 us -> 618 us (level)
    ppermute x45, waiting for transfers between devices: 187 us -> 196 us  [swap(): return lax.ppermute(value, 'shard', [(i, i ^ d) for i in range(n)])]
    unnamed x201 -> x197, local copies, waits for them, and re-layouts: 26.8 us -> 27.8 us
  transfers between devices with their start and end apart: 62 -> 62, of which waited for: 28 -> 28; matrix products, arithmetic and copies ran while one was open for 29% -> 29% of each run, Pallas kernels for 11% -> 10%
where the time goes in v3:
time: 618 us; the launch traced here: 609 us
  waiting for transfers between devices  240 us (39%)
  matrix products  120 us (19%)
  Pallas kernels  72.2 us (12%)
  starting transfers between devices  57.6 us (9%)
  local copies, waits for them, and re-layouts  52.1 us (8%)
  other arithmetic  51.7 us (8%)
  between operations  15.4 us (2%)
    ppermute x45, waiting for transfers between devices, swap(): return lax.ppermute(value, 'shard', [(i, i ^ d) for i in range(n)])  196 us
    dot_general x15, matrix products, dot(): lax.dot_general(left, right, (dims, ((), ())), preferred_element_type=F32)  69 us
    ppermute x45, starting transfers between devices, swap(): return lax.ppermute(value, 'shard', [(i, i ^ d) for i in range(n)])  52.9 us
    pallas_call x2, Pallas kernels, vmem_call(): pl.pallas_call(kernel, out_shape=out_shape, in_specs=[pl.BlockSpec(memory...  41.3 us
    pallas_call x7, Pallas kernels, local_call(): pl.pallas_call(kernel, out_shape=out_shape, in_specs=[pl.BlockSpec(memory...  30.9 us
    unnamed x197, local copies, waits for them, and re-layouts  27.8 us
    psum x1, waiting for transfers between devices, body(): attn_sum = lax.psum(after(attn_parts, fc_sum), 'plane')  20.4 us
    dot_general x4, matrix products, body(): jnp.dot(block(late_active, d), out_weight, preferred_element_type=F32)  18.7 us
  transfers between devices with their start and end apart: 62, of which 28 were waited for; matrix products, arithmetic and copies ran while one was open for 29% of the time, Pallas kernels for 10%

profile of v3, /device:TPU:0, one launch (start us, length us, event | category | flops | bytes accessed | tf_op | source)
XLA Modules:
  0.0 609.1 jit_solution(13399269853748045146)
XLA Ops:
  27.8 17.4 %collective-permute-done.refs_1_ = bf16[224,1344]{1,0:T(8,128)(2,1)S(1)} collective-permute-done((bf16[224,1344]{1,0:T(8,128)(2,1)}, bf16[224,1344]{1,0:T(8,128)(2,1)S(1)}, u32[]{:S(2)}, u32[]{:S(2)}) %collective-permute-start) | collective-permute-done | bytes 602144 | tf_op jit(solution)/shard_map/ppermute | solution.py:433
  45.2 11.8 %collective-permute-done.2.refs_3_ = bf16[224,1344]{1,0:T(8,128)(2,1)S(1)} collective-permute-done((bf16[224,1344]{1,0:T(8,128)(2,1)}, bf16[224,1344]{1,0:T(8,128)(2,1)S(1)}, u32[]{:S(2)}, u32[]{:S(2)}) %collective-permute-start.2) | collective-permute-done | bytes 602144 | tf_op jit(solution)/shard_map/ppermute | solution.py:433
  74.4 18.6 %collective-permute-done.5 = bf16[128,1600]{0,1:T(8,128)(2,1)S(1)} collective-permute-done((bf16[128,1600]{0,1:T(8,128)(2,1)}, bf16[128,1600]{0,1:T(8,128)(2,1)S(1)}, u32[]{:S(2)}, u32[]{:S(2)}) %collective-permute-start.5) | collective-permute-done | bytes 409632 | tf_op jit(solution)/shard_map/ppermute | solution.py:433
  100.8 9.3 %add_convert_fusion.qkv_ref = bf16[1024,1344]{1,0:T(8,128)(2,1)S(1)} fusion(bf16[1600,1344]{1,0:T(8,128)(2,1)} %get-tuple-element.99, f32[1344]{0:T(1024)S(1)} %concatenate.72, bf16[1024,1600]{0,1:T(8,128)(2,1)} %copy-done.25, f32[1600]{0:T(1024)S(1)} %get-tuple-element.175, f32[1600]{0:T(1024)S(1)} %get-tuple-element.176, f32[1024]{0:T(1024)S(1)} %add_rsqrt_fusion, ...), kind=kOutput, calls=%fused_computation.14 | convolution fusion | flops 4416602112 | bytes 10356480 | tf_op jit(solution)/shard_map/dot_general | solution.py:577
  116.7 13.1 %shard_map.274 = bf16[1024,448]{1,0:T(8,128)(2,1)S(1)} custom-call(s32[4]{0:T(128)S(1)} %pad_add_fusion.1.info_ref, bf16[1024,1344]{1,0:T(8,128)(2,1)S(1)} %add_convert_fusion.qkv_ref), custom_call_target="tpu_custom_call" | custom-call | flops 1 | bytes 1 | tf_op jit(solution)/shard_map/pallas_call | solution.py:200
  145.2 7.3 %collective-permute-done.20 = bf16[112,1600]{1,0:T(8,128)(2,1)S(1)} collective-permute-done((bf16[112,1600]{1,0:T(8,128)(2,1)S(1)}, bf16[112,1600]{1,0:T(8,128)(2,1)S(1)}, u32[]{:S(2)}, u32[]{:S(2)}) %collective-permute-start.20) | collective-permute-done | bytes 358432 | tf_op jit(solution)/shard_map/ppermute | solution.py:433
  172.0 6.4 %collective-permute-done.21.near = bf16[336,1600]{1,0:T(8,128)(2,1)S(1)} collective-permute-done((bf16[336,1600]{1,0:T(8,128)(2,1)S(1)}, bf16[336,1600]{1,0:T(8,128)(2,1)S(1)}, u32[]{:S(2)}, u32[]{:S(2)}) %collective-permute-start.21) | collective-permute-done | bytes 1075232 | tf_op jit(solution)/shard_map/ppermute | solution.py:436
  179.7 10.8 %convolution_convert_fusion.4 = bf16[1024,1600]{0,1:T(8,128)(2,1)} fusion(bf16[1600,1600]{1,0:T(8,128)(2,1)} %param.30, bf16[256,1600]{0,1:T(8,128)(2,1)S(1)} %get-tuple-element.186, bf16[256,1600]{0,1:T(8,128)(2,1)S(1)} %get-tuple-element.187, bf16[256,1600]{0,1:T(8,128)(2,1)S(1)} %get-tuple-element.185, bf16[256,1600]{0,1:T(8,128)(2,1)S(1)} %bitcast.161), kind=kOutput, calls=%fused_computation.19 | convolution fusion | flops 5257625600 | bytes 11673600 | tf_op jit(solution)/shard_map/dot_general | solution.py:23
  194.8 8.0 %collective-permute-done.23 = bf16[128,1600]{0,1:T(8,128)(2,1)S(1)} collective-permute-done((bf16[128,1600]{0,1:T(8,128)(2,1)S(1)}, bf16[128,1600]{0,1:T(8,128)(2,1)S(1)}, u32[]{:S(2)}, u32[]{:S(2)}) %collective-permute-start.23) | collective-permute-done | bytes 409632 | tf_op jit(solution)/shard_map/ppermute | solution.py:433
  207.8 6.5 %multiply_convert_fusion.5 = (bf16[256,1600]{0,1:T(8,128)(2,1)S(1)}, f32[256,1600]{0,1:T(8,128)}) fusion(f32[1600]{0:T(1024)S(1)} %copy-done.70, bf16[256,1600]{0,1:T(8,128)(2,1)S(1)} %collective-permute-done.19, bf16[1600,1600]{1,0:T(8,128)(2,1)} %shard_map.276), kind=kOutput, calls=%fused_computation.112 | convolution fusion | flops 1314816000 | bytes 8403200 | tf_op jit(solution)/shard_map/dot_general | solution.py:622
  226.5 8.8 %convolution_convert_fusion.2 = bf16[1600,1600]{1,0:T(8,128)(2,1)} fusion(bf16[256,1600]{0,1:T(8,128)(2,1)S(1)} %copy-done.55, bf16[256,1600]{0,1:T(8,128)(2,1)S(1)} %copy-done.57, bf16[256,1600]{0,1:T(8,128)(2,1)S(1)} %copy-done.53, bf16[256,1600]{0,1:T(8,128)(2,1)S(1)} %bitcast.162, bf16[256,1600]{0,1:T(8,128)(2,1)S(1)} %get-tuple-element.235, ...), kind=kOutput, calls=%fused_computation.6 | convolution fusion | flops 5271654400 | bytes 11673600 | tf_op jit(solution)/shard_map/dot_general | solution.py:23
  254.6 7.8 %convolution_convert_fusion.1 = bf16[1600,1600]{1,0:T(8,128)(2,1)S(1)} fusion(bf16[1024,1600]{0,1:T(8,128)(2,1)} %constant_dynamic-update-slice_fusion.8, bf16[256,1600]{0,1:T(8,128)(2,1)S(1)} %get-tuple-element.181, bf16[256,1600]{0,1:T(8,128)(2,1)S(1)} %get-tuple-element.182, bf16[256,1600]{0,1:T(8,128)(2,1)S(1)} %get-tuple-element.183, ...), kind=kOutput, calls=%fused_computation.5 | convolution fusion | flops 5258547200 | bytes 11673600 | tf_op jit(solution)/shard_map/dot_general | solution.py:23
  272.3 16.3 %collective-permute-done.26 = bf16[256,1600]{0,1:T(8,128)(2,1)S(1)} collective-permute-done((bf16[256,1600]{0,1:T(8,128)(2,1)S(1)}, bf16[256,1600]{0,1:T(8,128)(2,1)S(1)}, u32[]{:S(2)}, u32[]{:S(2)}) %collective-permute-start.26) | collective-permute-done | bytes 819232 | tf_op jit(solution)/shard_map/ppermute | solution.py:433
  321.3 28.2 %shard_map.277 = bf16[1024,1344]{1,0:T(8,128)(2,1)S(1)} custom-call(s32[4]{0:T(128)S(1)} %pad_add_fusion.1.info_ref, bf16[1024,1344]{1,0:T(8,128)(2,1)} %copy-done, bf16[1024,448]{1,0:T(8,128)(2,1)S(1)} %copy-done.1), custom_call_target="tpu_custom_call" | custom-call | flops 1 | bytes 1 | tf_op jit(solution)/shard_map/pallas_call | solution.py:200
  355.0 7.3 %convert_element_type.276 = f32[1600,1600]{1,0:T(8,128)} convert(bf16[1600,1600]{1,0:T(8,128)(2,1)} %all-reduce.4.cloned.1.call-done) | non-fusion elementwise | flops 2560000 | bytes 15360000 | tf_op jit(solution)/shard_map/convert_element_type | solution.py:662
  363.1 6.9 %convolution_convert_fusion = bf16[1600,1152]{1,0:T(8,128)(2,1)S(1)} fusion(bf16[1024,1344]{1,0:T(8,128)(2,1)S(1)} %shard_map.277, bf16[1024,1600]{0,1:T(8,128)(2,1)} %copy-done.25, f32[1600]{0:T(1024)S(1)} %copy-done.67, f32[1600]{0:T(1024)S(1)} %get-tuple-element.176, f32[1024]{0:T(1024)S(1)} %copy-done.75, f32[1024]{0:T(1024)S(1)} %broadcast_multiply_fusion), kind=kOutput, calls=%fused_computation.4 | convolution fusion | flops 3786547200 | bytes 9347072 | tf_op jit(solution)/shard_map/dot_general | solution.py:23
  388.5 12.3 %collective-permute-done.43 = bf16[208,1600]{1,0:T(8,128)(2,1)S(1)} collective-permute-done((bf16[208,1600]{1,0:T(8,128)(2,1)S(1)}, bf16[208,1600]{1,0:T(8,128)(2,1)S(1)}, u32[]{:S(2)}, u32[]{:S(2)}) %collective-permute-start.43) | collective-permute-done | bytes 665632 | tf_op jit(solution)/shard_map/ppermute | solution.py:433
  400.9 14.4 %collective-permute-done.42 = bf16[208,1600]{1,0:T(8,128)(2,1)S(1)} collective-permute-done((bf16[208,1600]{1,0:T(8,128)(2,1)S(1)}, bf16[208,1600]{1,0:T(8,128)(2,1)S(1)}, u32[]{:S(2)}, u32[]{:S(2)}) %collective-permute-start.42) | collective-permute-done | bytes 665632 | tf_op jit(solution)/shard_map/ppermute | solution.py:433
  421.4 10.9 %collective-permute-done.38 = bf16[208,1152]{1,0:T(8,128)(2,1)S(1)} collective-permute-done((bf16[208,1152]{1,0:T(8,128)(2,1)S(1)}, bf16[208,1152]{1,0:T(8,128)(2,1)S(1)}, u32[]{:S(2)}, u32[]{:S(2)}) %collective-permute-start.38) | collective-permute-done | bytes 479264 | tf_op jit(solution)/shard_map/ppermute | solution.py:433
  432.3 9.4 %collective-permute-done.37 = bf16[208,1152]{1,0:T(8,128)(2,1)S(1)} collective-permute-done((bf16[208,1152]{1,0:T(8,128)(2,1)S(1)}, bf16[208,1152]{1,0:T(8,128)(2,1)S(1)}, u32[]{:S(2)}, u32[]{:S(2)}) %collective-permute-start.37) | collective-permute-done | bytes 479264 | tf_op jit(solution)/shard_map/ppermute | solution.py:433
  483.4 14.7 %collective-permute-done.44 = bf16[256,1600]{0,1:T(8,128)(2,1)} collective-permute-done((bf16[256,1600]{0,1:T(8,128)(2,1)}, bf16[256,1600]{0,1:T(8,128)(2,1)}, u32[]{:S(2)}, u32[]{:S(2)}) %collective-permute-start.44) | collective-permute-done | bytes 819232 | tf_op jit(solution)/shard_map/ppermute | solution.py:433
  499.5 34.0 %collective-permute-done.45 = bf16[256,1600]{0,1:T(8,128)(2,1)} collective-permute-done((bf16[256,1600]{0,1:T(8,128)(2,1)}, bf16[256,1600]{0,1:T(8,128)(2,1)}, u32[]{:S(2)}, u32[]{:S(2)}) %collective-permute-start.45) | collective-permute-done | bytes 819232 | tf_op jit(solution)/shard_map/ppermute | solution.py:433
  533.5 6.7 %fusion.18 = (f32[256]{0:T(256)S(1)}, f32[1600]{0:T(1024)S(1)}, f32[256]{0:T(256)S(1)}, f32[1600]{0:T(1024)S(1)}, f32[256,1600]{0,1:T(8,128)}) fusion(f32[1600]{0:T(1024)S(1)} %get-tuple-element.176, f32[256]{0:T(256)S(1)} %copy-done.76, f32[256]{0:T(256)S(1)} %copy-done.65, bf16[1,256,1600]{1,2,0:T(8,128)(2,1)} %param.16, ...), kind=kOutput, calls=%fused_computation.69 | convolution fusion | flops 1107554816 | bytes 10164992 | tf_op jit(solution)/shard_map/dot_general | solution.py:23
  569.1 20.4 %all-reduce.8.cloned.1.call-done.refs_0_ = bf16[208,6400]{1,0:T(8,128)(2,1)} async-done(((bf16[208,6400]{1,0:T(8,128)(2,1)}), bf16[208,6400]{1,0:T(8,128)(2,1)}) %all-reduce.8.cloned.1.call-update) | async-done | bytes 2662416 | tf_op jit(solution)/shard_map/psum | solution.py:682
  (443 shorter events, 286.6 us)
Async XLA Ops:
  7.2 153.4 %all-gather.2.cloned.1.call-start = ((), (), s32[]{:S(2)}) async-start(), calls=%async_computation | async-start | bytes 4096000 | tf_op jit(solution)/shard_map/all_gather | solution.py:557
  7.2 49.8 %collective-permute-start.4 = (bf16[256,1600]{0,1:T(8,128)(2,1)}, bf16[256,1600]{0,1:T(8,128)(2,1)}, u32[]{:S(2)}, u32[]{:S(2)}) collective-permute-start(bf16[256,1600]{0,1:T(8,128)(2,1)} %bitcast.150), channel_id=1, source_target_pairs={{0,16},{8,24},{16,0},{24,8},{1,17},{9,25},{17,1},{25,9},{2,18},{10... | collective-permute-start | bytes 2457608 | tf_op jit(solution)/shard_map/ppermute | solution.py:433
  10.3 46.8 %collective-permute-start.3 = (bf16[256,1600]{0,1:T(8,128)(2,1)}, bf16[256,1600]{0,1:T(8,128)(2,1)}, u32[]{:S(2)}, u32[]{:S(2)}) collective-permute-start(bf16[256,1600]{0,1:T(8,128)(2,1)} %bitcast.151), channel_id=1, source_target_pairs={{0,8},{8,0},{16,24},{24,16},{1,9},{9,1},{17,25},{25,17},{2,10},{10... | collective-permute-start | bytes 2457608 | tf_op jit(solution)/shard_map/ppermute | solution.py:433
  22.8 34.2 %collective-permute-start.2 = (bf16[224,1344]{1,0:T(8,128)(2,1)}, bf16[224,1344]{1,0:T(8,128)(2,1)S(1)}, u32[]{:S(2)}, u32[]{:S(2)}) collective-permute-start(bf16[224,1344]{1,0:T(8,128)(2,1)} %get-tuple-element.91), channel_id=1, source_target_pairs={{0,24},{8,16},{16,8},{24,0},{1,25},{9,17},{17,9},{25,1},{2,26},{10... | collective-permute-start | bytes 1806344 | tf_op jit(solution)/shard_map/ppermute | solution.py:433
  58.8 51.4 %collective-permute-start.9 = (bf16[208,1600]{1,0:T(8,128)(2,1)}, bf16[208,1600]{1,0:T(8,128)(2,1)}, u32[]{:S(2)}, u32[]{:S(2)}) collective-permute-start(bf16[208,1600]{1,0:T(8,128)(2,1)} %constant_dynamic-slice_fusion.11), channel_id=1, source_target_pairs={{0,16},{8,24},{16,0},{24,8},{1,17},{9,25},{17,1},{25,9},{2,18},{10... | collective-permute-start | bytes 1996808 | tf_op jit(solution)/shard_map/ppermute | solution.py:433
  60.4 49.7 %collective-permute-start.8 = (bf16[208,1600]{1,0:T(8,128)(2,1)}, bf16[208,1600]{1,0:T(8,128)(2,1)}, u32[]{:S(2)}, u32[]{:S(2)}) collective-permute-start(bf16[208,1600]{1,0:T(8,128)(2,1)} %constant_dynamic-slice_fusion.11), channel_id=1, source_target_pairs={{0,8},{8,0},{16,24},{24,16},{1,9},{9,1},{17,25},{25,17},{2,10},{10... | collective-permute-start | bytes 1996808 | tf_op jit(solution)/shard_map/ppermute | solution.py:433
  64.9 290.1 %all-reduce.4.cloned.1.call-start = ((), (), s32[]{:S(2)}) async-start(), calls=%async_computation.1 | async-start | bytes 10649600 | tf_op jit(solution)/shard_map/psum | solution.py:634
  235.3 248.1 %all-reduce.6.cloned.1.call-start = ((), (), s32[]{:S(2)}) async-start(), calls=%async_computation.2 | async-start | bytes 5537792 | tf_op jit(solution)/shard_map/psum | solution.py:661
  252.8 35.9 %collective-permute-start.26 = (bf16[256,1600]{0,1:T(8,128)(2,1)S(1)}, bf16[256,1600]{0,1:T(8,128)(2,1)S(1)}, u32[]{:S(2)}, u32[]{:S(2)}) collective-permute-start(bf16[256,1600]{0,1:T(8,128)(2,1)S(1)} %convolution_convert_fusion.9), channel_id=1, source_target_pairs={{0,16},{8,24},{16,0},{24,8},{1,17},{9,25},{17,1},{25,9},{2,18},{10... | collective-permute-start | bytes 2457608 | tf_op jit(solution)/shard_map/ppermute | solution.py:433
  254.3 35.1 %collective-permute-start.27 = (bf16[256,1600]{0,1:T(8,128)(2,1)S(1)}, bf16[256,1600]{0,1:T(8,128)(2,1)S(1)}, u32[]{:S(2)}, u32[]{:S(2)}) collective-permute-start(bf16[256,1600]{0,1:T(8,128)(2,1)S(1)} %convolution_convert_fusion.8), channel_id=1, source_target_pairs={{0,24},{8,16},{16,8},{24,0},{1,25},{9,17},{17,9},{25,1},{2,26},{10... | collective-permute-start | bytes 2457608 | tf_op jit(solution)/shard_map/ppermute | solution.py:433
  262.7 38.8 %collective-permute-start.31 = (bf16[4,208,1600]{2,1,0:T(8,128)(2,1)S(1)}, bf16[4,208,1600]{2,1,0:T(8,128)(2,1)S(1)}, u32[]{:S(2)}, u32[]{:S(2)}) collective-permute-start(bf16[4,208,1600]{2,1,0:T(8,128)(2,1)S(1)} %constant_dynamic-slice_fusion.7), channel_id=1, source_target_pairs={{0,1},{1,0},{2,3},{3,2},{4,5},{5,4},{6,7},{7,6},{8,9},{9,8},{10,11... | collective-permute-start | bytes 7987208 | tf_op jit(solution)/shard_map/ppermute | solution.py:439
  311.5 38.1 %collective-permute-start.34 = (bf16[208,1600]{1,0:T(8,128)(2,1)}, bf16[208,1600]{1,0:T(8,128)(2,1)}, u32[]{:S(2)}, u32[]{:S(2)}) collective-permute-start(bf16[208,1600]{1,0:T(8,128)(2,1)} %get-tuple-element.192), channel_id=1, source_target_pairs={{0,24},{8,16},{16,8},{24,0},{1,25},{9,17},{17,9},{25,1},{2,26},{10... | collective-permute-start | bytes 1996808 | tf_op jit(solution)/shard_map/ppermute | solution.py:433
  313.0 36.5 %collective-permute-start.33 = (bf16[208,1600]{1,0:T(8,128)(2,1)}, bf16[208,1600]{1,0:T(8,128)(2,1)}, u32[]{:S(2)}, u32[]{:S(2)}) collective-permute-start(bf16[208,1600]{1,0:T(8,128)(2,1)} %get-tuple-element.193), channel_id=1, source_target_pairs={{0,16},{8,24},{16,0},{24,8},{1,17},{9,25},{17,1},{25,9},{2,18},{10... | collective-permute-start | bytes 1996808 | tf_op jit(solution)/shard_map/ppermute | solution.py:433
  313.5 36.1 %collective-permute-start.32 = (bf16[208,1600]{1,0:T(8,128)(2,1)}, bf16[208,1600]{1,0:T(8,128)(2,1)}, u32[]{:S(2)}, u32[]{:S(2)}) collective-permute-start(bf16[208,1600]{1,0:T(8,128)(2,1)} %get-tuple-element.194), channel_id=1, source_target_pairs={{0,8},{8,0},{16,24},{24,16},{1,9},{9,1},{17,25},{25,17},{2,10},{10... | collective-permute-start | bytes 1996808 | tf_op jit(solution)/shard_map/ppermute | solution.py:433
  316.8 61.1 %collective-permute-start.40 = (bf16[4,208,1600]{2,1,0:T(8,128)(2,1)}, bf16[4,208,1600]{2,1,0:T(8,128)(2,1)}, u32[]{:S(2)}, u32[]{:S(2)}) collective-permute-start(bf16[4,208,1600]{2,1,0:T(8,128)(2,1)} %constant_dynamic-slice_fusion.4), channel_id=1, source_target_pairs={{0,1},{1,0},{2,3},{3,2},{4,5},{5,4},{6,7},{7,6},{8,9},{9,8},{10,11... | collective-permute-start | bytes 7987208 | tf_op jit(solution)/shard_map/ppermute | solution.py:439
  362.4 227.1 %all-reduce.8.cloned.1.call-start = ((), (), s32[]{:S(2)}) async-start(), calls=%async_computation.3 | async-start | bytes 5324800 | tf_op jit(solution)/shard_map/psum | solution.py:682
  373.2 42.1 %collective-permute-start.35 = (bf16[4,208,1152]{2,1,0:T(8,128)(2,1)}, bf16[4,208,1152]{2,1,0:T(8,128)(2,1)}, u32[]{:S(2)}, u32[]{:S(2)}) collective-permute-start(bf16[4,208,1152]{2,1,0:T(8,128)(2,1)} %constant_dynamic-slice_fusion.6), channel_id=1, source_target_pairs={{0,1},{1,0},{2,3},{3,2},{4,5},{5,4},{6,7},{7,6},{8,9},{9,8},{10,11... | collective-permute-start | bytes 5750792 | tf_op jit(solution)/shard_map/ppermute | solution.py:439
  383.9 31.4 %collective-permute-start.42 = (bf16[208,1600]{1,0:T(8,128)(2,1)S(1)}, bf16[208,1600]{1,0:T(8,128)(2,1)S(1)}, u32[]{:S(2)}, u32[]{:S(2)}) collective-permute-start(bf16[208,1600]{1,0:T(8,128)(2,1)S(1)} %get-tuple-element.189), channel_id=1, source_target_pairs={{0,16},{8,24},{16,0},{24,8},{1,17},{9,25},{17,1},{25,9},{2,18},{10... | collective-permute-start | bytes 1996808 | tf_op jit(solution)/shard_map/ppermute | solution.py:433
  459.1 81.3 %collective-permute-start.53 = (bf16[256,1600]{0,1:T(8,128)(2,1)}, bf16[256,1600]{0,1:T(8,128)(2,1)}, u32[]{:S(2)}, u32[]{:S(2)}) collective-permute-start(bf16[256,1600]{0,1:T(8,128)(2,1)} %convolution_convert_fusion.13), channel_id=1, source_target_pairs={{0,8},{8,0},{16,24},{24,16},{1,9},{9,1},{17,25},{25,17},{2,10},{10... | collective-permute-start | bytes 2457608 | tf_op jit(solution)/shard_map/ppermute | solution.py:433
  460.5 79.9 %collective-permute-start.54 = (bf16[256,1600]{0,1:T(8,128)(2,1)}, bf16[256,1600]{0,1:T(8,128)(2,1)}, u32[]{:S(2)}, u32[]{:S(2)}) collective-permute-start(bf16[256,1600]{0,1:T(8,128)(2,1)} %convolution_convert_fusion.12), channel_id=1, source_target_pairs={{0,16},{8,24},{16,0},{24,8},{1,17},{9,25},{17,1},{25,9},{2,18},{10... | collective-permute-start | bytes 2457608 | tf_op jit(solution)/shard_map/ppermute | solution.py:433
  465.9 32.2 %collective-permute-start.44 = (bf16[256,1600]{0,1:T(8,128)(2,1)}, bf16[256,1600]{0,1:T(8,128)(2,1)}, u32[]{:S(2)}, u32[]{:S(2)}) collective-permute-start(bf16[256,1600]{0,1:T(8,128)(2,1)} %convolution_convert_fusion.7), channel_id=1, source_target_pairs={{0,8},{8,0},{16,24},{24,16},{1,9},{9,1},{17,25},{25,17},{2,10},{10... | collective-permute-start | bytes 2457608 | tf_op jit(solution)/shard_map/ppermute | solution.py:433
  472.2 61.3 %collective-permute-start.45 = (bf16[256,1600]{0,1:T(8,128)(2,1)}, bf16[256,1600]{0,1:T(8,128)(2,1)}, u32[]{:S(2)}, u32[]{:S(2)}) collective-permute-start(bf16[256,1600]{0,1:T(8,128)(2,1)} %convolution_convert_fusion.6), channel_id=1, source_target_pairs={{0,16},{8,24},{16,0},{24,8},{1,17},{9,25},{17,1},{25,9},{2,18},{10... | collective-permute-start | bytes 2457608 | tf_op jit(solution)/shard_map/ppermute | solution.py:433
  475.3 58.2 %collective-permute-start.46 = (bf16[256,1600]{0,1:T(8,128)(2,1)}, bf16[256,1600]{0,1:T(8,128)(2,1)}, u32[]{:S(2)}, u32[]{:S(2)}) collective-permute-start(bf16[256,1600]{0,1:T(8,128)(2,1)} %convolution_convert_fusion.5), channel_id=1, source_target_pairs={{0,24},{8,16},{16,8},{24,0},{1,25},{9,17},{17,9},{25,1},{2,26},{10... | collective-permute-start | bytes 2457608 | tf_op jit(solution)/shard_map/ppermute | solution.py:433
  498.1 42.4 %collective-permute-start.55 = (bf16[256,1600]{0,1:T(8,128)(2,1)}, bf16[256,1600]{0,1:T(8,128)(2,1)}, u32[]{:S(2)}, u32[]{:S(2)}) collective-permute-start(bf16[256,1600]{0,1:T(8,128)(2,1)} %convolution_convert_fusion.11), channel_id=1, source_target_pairs={{0,24},{8,16},{16,8},{24,0},{1,25},{9,17},{17,9},{25,1},{2,26},{10... | collective-permute-start | bytes 2457608 | tf_op jit(solution)/shard_map/ppermute | solution.py:433
  (125 other events, 1723.0 us)
Sparse Core Ops, SparseCore 0:
  65.0 57.4 all-gather.1
  235.4 119.5 all-reduce.3
  362.5 108.8 all-reduce.5
  483.5 105.8 all-reduce.7
